TPU v7x, 512 devices: a whole 4x4x16 slice. The times are simulated.
512 devices in a mesh: dp: 32 (over x, y, core), seq: 16 (over z).
Axes of the slice: x: 4, y: 4, z: 16, core: 2. Of those that a mesh axis runs over, the one named last changes fastest.
Arguments:
- tile_tokens: bfloat16 [32, 512, 3200], P('dp', 'seq'), may hold values from -6 to 6
- proj_weight: bfloat16 [3200, 8192], P('dp', 'seq')
- text_hidden: bfloat16 [32, 2048, 8192], P('dp', 'seq'), may hold values from -6 to 6
- cotangent: bfloat16 [32, 2048, 8192], P('dp', 'seq'), may hold values from -1.1953125 to 1.1953125
- norm_gain: float32 [8192], replicated, may hold values from 0.25 to 1.75
- placeholders: int32 [32, 512], P('dp'), may hold values from 0 to 2047, as said below
- bucket_levels: int32 [32, 16, 3200], P('dp', 'seq'), may hold values from 2 to 16
- row_draws: float32 [32, 16, 3200], P('dp', 'seq'), may hold values from 0 to 1
- column_draws: float32 [32, 8192], P('dp', 'seq'), may hold values from 0 to 1
Outputs:
- weight_grad: float32 [3200, 8192], P('dp', 'seq')
- gain_grad: float32 [8192], replicated
Inputs may be any that keep to these rules, and one draw needn't show every extreme that they name: Each row is strictly increasing. Among the positions of one device's block of 128 positions stand at most 48 placeholders, and in every row some block holds exactly 48.
All inputs are finite; a program needn't handle non-finite values.
Results may differ from a plain program's by a relative error of at most 0.014.
Values may be sent and summed in bfloat16 or wider, within the bound.
A program may use at most 64 MiB of HBM per device.

v0:
```python
import jax
import jax.numpy as jnp
from jax import lax
from jax.sharding import Mesh
from jax.sharding import PartitionSpec as P

IMG_MOST = 48
DP = ("dp_0", "dp_1", "dp_2")
DP_SEQ = ("dp_0", "dp_1", "dp_2", "seq")


EPSILON = 1e-06


def copy_for_each(value, axis):
    copies = jnp.broadcast_to(value, (lax.axis_size(axis), *value.shape))
    return lax.all_to_all(copies, axis, split_axis=0, concat_axis=0, tiled=True)


def of_everyone(value, axis):
    everything = copy_for_each(value, axis)
    return jnp.sum(everything, axis=0)


def in_one(arrays, axis):
    ravelled, at, outs = (jnp.concatenate([a.reshape(-1) for a in arrays]), 0, [])
    so_far = of_everyone(ravelled, axis)
    for a in arrays:
        outs.append(so_far[at : at + a.size].reshape(a.shape))
        at += a.size
    return tuple(outs)


def one_axis_at_a_time(value, axes):
    for axis in axes:
        value = lax.psum(value, axis)
    return value


def quantize(gradient, levels_now, rows_now, columns_now):
    bucket_norm = jnp.sqrt(jnp.sum(gradient * gradient, axis=1, keepdims=True) + EPSILON)
    step_count = levels_now.astype(jnp.float32)[:, None]
    offset = 0.25 + 0.25 * (rows_now[:, None] + columns_now[None, :])
    ratio = jnp.abs(gradient) / bucket_norm * step_count
    lower = jnp.floor(ratio)
    quantum = lower + jnp.clip(2.0 * (ratio - lower - offset) + 0.5, 0.0, 1.0)
    return jnp.sign(gradient) * bucket_norm * quantum / step_count


def on_device(
    tile_tokens,
    proj_weight,
    text_hidden,
    cotangent,
    norm_gain,
    placeholders,
    bucket_levels,
    row_draws,
    column_draws,
):
    seq_count = lax.axis_size("seq")
    seq_index = lax.axis_index("seq")
    replicas = lax.axis_size(DP)
    places = placeholders[0]
    image_total = places.shape[0]
    tok_rows = text_hidden.shape[1]
    model_width = text_hidden.shape[2]
    columns = proj_weight.shape[1]
    all_positions = tok_rows * seq_count
    zero_half = jnp.zeros((), jnp.bfloat16)
    own_text = text_hidden[0]
    own_cot = cotangent[0]
    gathered = lax.all_gather(tile_tokens[0], "seq", axis=0, tiled=True)
    patch_block = gathered
    embedded = jnp.dot(
        patch_block,
        lax.all_gather(proj_weight, DP, axis=0, tiled=True),
        preferred_element_type=jnp.float32,
    ).astype(jnp.bfloat16)
    image_marks = jnp.zeros((all_positions,), jnp.int32).at[places].set(1)
    local_marks = lax.dynamic_slice_in_dim(image_marks, seq_index * tok_rows, tok_rows)
    is_image = local_marks[:, None] == 1
    owners = places // tok_rows
    owner_ids = jnp.arange(seq_count, dtype=jnp.int32)
    counts = jnp.sum((owners[:, None] == owner_ids[None, :]).astype(jnp.int32), axis=0)
    starts = jnp.cumsum(counts) - counts
    own_start = starts[seq_index]
    own_count = counts[seq_index]
    slot_ids = jnp.arange(IMG_MOST, dtype=jnp.int32)
    source_rows = jnp.clip(own_start + slot_ids, 0, image_total - 1)
    local_slots = jnp.clip(jnp.take(places, source_rows) - seq_index * tok_rows, 0, tok_rows - 1)
    slot_live = (slot_ids < own_count)[:, None]
    flat_index = owners * IMG_MOST + (
        jnp.arange(image_total, dtype=jnp.int32) - jnp.take(starts, owners)
    )
    outgoing = jnp.where(slot_live, jnp.take(own_cot, local_slots, axis=0), zero_half)
    returned = lax.all_to_all(outgoing[None], "seq", split_axis=2, concat_axis=0, tiled=True)
    image_cot = jnp.take(returned.reshape(-1, columns), flat_index, axis=0).astype(jnp.float32)
    emb_float = embedded.astype(jnp.float32)
    column_gain = lax.dynamic_slice_in_dim(norm_gain, seq_index * columns, columns)
    grad_in = image_cot * column_gain[None, :]
    squares, mixed = in_one(
        (jnp.sum(emb_float * emb_float, axis=1), jnp.sum(grad_in * emb_float, axis=1)), "seq"
    )
    inverse = lax.rsqrt(squares / model_width + EPSILON)[:, None]
    normed = emb_float * inverse
    emb_grad = ((grad_in - normed * (mixed[:, None] * inverse / model_width)) * inverse).astype(
        jnp.bfloat16
    )
    image_part = jnp.sum(image_cot * normed, axis=0)
    text_float = own_text.astype(jnp.float32)
    text_inverse = lax.rsqrt(jnp.mean(text_float * text_float, axis=1, keepdims=True) + EPSILON)
    text_terms = own_cot.astype(jnp.float32) * text_float * text_inverse
    text_part = jnp.sum(jnp.where(is_image, 0.0, text_terms), axis=0)
    placed_part = lax.dynamic_update_slice_in_dim(
        jnp.zeros((model_width,), jnp.float32), image_part, seq_index * columns, 0
    )
    gain_part = text_part + placed_part
    own_levels = bucket_levels[0, 0]
    own_row_draws = row_draws[0, 0]
    own_column_draws = column_draws[0]
    patch_block = gathered
    gradient = lax.dot_general(
        patch_block, emb_grad, (((0,), (0,)), ((), ())), preferred_element_type=jnp.float32
    )
    summed = lax.psum_scatter(
        quantize(gradient, own_levels, own_row_draws, own_column_draws).astype(jnp.bfloat16),
        DP,
        scatter_dimension=0,
        tiled=True,
    ).astype(jnp.float32)
    gain_total = one_axis_at_a_time(gain_part, DP_SEQ)
    return (summed / replicas, gain_total / replicas)


def solution(mesh):
    finer = Mesh(mesh.devices.reshape(4, 4, 2, mesh.shape["seq"]), ("dp_0", "dp_1", "dp_2", "seq"))
    return jax.shard_map(
        on_device,
        mesh=finer,
        in_specs=(
            P(DP, "seq", None),
            P(DP, "seq"),
            P(DP, "seq", None),
            P(DP, "seq", None),
            P(),
            P(DP, None),
            P(DP, "seq", None),
            P(DP, "seq", None),
            P(DP, "seq"),
        ),
        out_specs=(P(DP, "seq"), P()),
        check_vma=False,
    )
```

profile of v0, /device:TPU:1, one launch (start us, length us, event | category | flops | bytes accessed | tf_op | source)
XLA Modules:
  0.0 358.7 jit_solution(13340607720197606231)
XLA Ops:
  7.2 0.7 all-gather.7.cloned.1.call-update
  7.9 0.7 all-gather.5.cloned.1.call-update
  8.6 0.7 add_select_fusion
  9.7 0.6 dynamic_slice.12
  10.3 0.7 fusion.39
  11.1 0.7 fusion.37
  11.8 1.5 gather_fusion
  13.2 0.7 fusion.36
  13.9 3.6 %gather_fusion.1 = bf16[48,8192]{1,0:T(8,128)(2,1)S(1)} fusion(bf16[128,8192]{1,0:T(8,128)(2,1)} %bitcast.91, s32[1024]{0:T(1024)S(1)} %pad_clamp_fusion.1), kind=kCustom, calls=%fused_computation.1 | custom fusion | bytes 1573056 | tf_op jit(solution)/shard_map/jit(_take)/gather | solution.py:96
  17.6 1.3 compare_and_fusion
  18.9 0.2 fusion.25
  19.0 6.8 %copy.37 = bf16[1,48,8192]{1,0,2:T(2,128)(2,1)} copy(bf16[1,48,8192]{2,1,0:T(8,128)(2,1)S(1)} %fusion.25) | data formatting | bytes 1572864 | tf_op jit(solution)/shard_map/jit(_where)/select_n | solution.py:96
  25.9 0.5 broadcast.663
  26.4 45.1 %reduce.24 = bf16[8192,48]{1,0:T(8,128)(2,1)S(1)} reduce(bf16[8192,1,48]{2,1,0:T(2,128)(2,1)} %bitcast.93, bf16[]{:T(256)} %broadcast.663), dimensions={1}, to_apply=%bitcast.79.reduce_sub_computation | reduce | bytes 1572866
  71.5 3.9 %reshape.481 = bf16[16,2,12288]{2,1,0:T(2,128)(2,1)} reshape(bf16[8192,48]{1,0:T(8,128)(2,1)S(1)} %reduce.24) | data formatting | bytes 1572864
  75.4 15.8 %all-to-all-start = ((bf16[16,2,12288]{2,1,0:T(2,128)(2,1)}), bf16[16,2,12288]{2,1,0:T(2,128)(2,1)S(1)}, u32[]{:S(2)}, u32[]{:S(2)}) async-start(bf16[16,2,12288]{2,1,0:T(2,128)(2,1)} %reshape.481), calls=%async_computation | async-start | bytes 1572864 | tf_op jit(solution)/shard_map/all_to_all | solution.py:97
  91.2 0.8 dynamic_slice.14
  92.0 4.3 %compare_select_fusion.2 = (s32[512,1]{0,1:T(1,128)S(1)}, s32[512,1]{0,1:T(1,128)S(1)}, s32[512,1]{0,1:T(1,128)S(1)}, s32[512,1]{0,1:T(1,128)S(1)}) fusion(s32[]{:T(128)} %bitcast.12, s32[]{:T(128)} %bitcast.13, s32[]{:T(128)} %bitcast.14, s32[]{:T(128)} %bitcast.15, s32[]{:T(128)} %bitcast.16, s32[]{:T(128)} %bitcast.18, s32[]{:T(128)} %bitcast.17, ...), kind=kLoop, calls=%fused_computation.62 | loop fusion | flops 16384 | bytes 10268 | tf_op jit(solution)/shard_map/jit(_take)/gather | solution.py:94
  96.3 5.8 %compare_and_fusion.1 = (pred[512]{0:T(512)(128)(4,1)S(1)}, s32[512]{0:T(512)S(1)}) fusion(pred[512]{0:T(512)(128)(4,1)S(1)} %get-tuple-element.24, pred[512]{0:T(512)(128)(4,1)S(1)} %get-tuple-element.22, pred[512]{0:T(512)(128)(4,1)S(1)} %get-tuple-element.23, pred[512]{0:T(512)(128)(4,1)S(1)} %get-tuple-element.21, ...), kind=kLoop, calls=%fused_computation.102 | loop fusion | flops 20480 | bytes 11300 | tf_op jit(solution)/shard_map/jit(_take)/and | solution.py:98
  102.2 29.5 %all-to-all-done = bf16[16,2,12288]{2,1,0:T(2,128)(2,1)S(1)} async-done(((bf16[16,2,12288]{2,1,0:T(2,128)(2,1)}), bf16[16,2,12288]{2,1,0:T(2,128)(2,1)S(1)}, u32[]{:S(2)}, u32[]{:S(2)}) %all-to-all-start) | async-done | bytes 786464 | tf_op jit(solution)/shard_map/all_to_all | solution.py:97
  131.7 7.9 %reshape.482 = bf16[8192,1,48]{2,1,0:T(2,128)(2,1)} reshape(bf16[16,2,12288]{2,1,0:T(2,128)(2,1)S(1)} %all-to-all-done) | data formatting | bytes 1572864
  139.6 8.1 %copy.38 = bf16[1,48,8192]{2,1,0:T(8,128)(2,1)S(1)} copy(bf16[1,48,8192]{1,0,2:T(2,128)(2,1)} %bitcast.94) | data formatting | bytes 1572864 | tf_op jit(solution)/shard_map/all_to_all | solution.py:97
  147.7 0.2 copy.48
  148.0 0.4 copy.39
  148.5 2.0 gather_fusion.2
  150.5 1.0 copy.40
  151.5 3.7 %reshape.455 = bf16[3200,512]{1,0:T(8,128)(2,1)S(1)} reshape(bf16[32,100,512]{2,1,0:T(8,128)(2,1)} %all-gather.7.cloned.1.call-done) | data formatting | bytes 6553600
  155.2 19.1 %all-gather.5.cloned.1.call-done = bf16[1,512,3200]{2,1,0:T(8,128)(2,1)} async-done(((bf16[1,32,3200]{2,1,0:T(8,128)(2,1)}), bf16[1,512,3200]{2,1,0:T(8,128)(2,1)}) %all-gather.5.cloned.1.call-update) | async-done | bytes 3276816 | tf_op jit(solution)/shard_map/all_gather | solution.py:73
  174.3 4.9 %fusion.23 = (f32[512]{0:T(512)S(1)}, f32[512]{0:T(512)S(1)}, bf16[512,512]{0,1:T(8,128)(2,1)}) fusion(f32[512]{0:T(512)S(1)} %dynamic_slice.14, bf16[512,512]{0,1:T(8,128)(2,1)} %copy.40, pred[512]{0:T(512)(128)(4,1)S(1)} %get-tuple-element.25, bf16[3200,512]{1,0:T(8,128)(2,1)S(1)} %reshape.455, bf16[1,512,3200]{2,1,0:T(8,128)(2,1)} %all-gather.5.cloned.1.call-done), kind=kOutput, calls=%fused_computation.35 | convolution fusion | flops 1680079872 | bytes 7608832 | tf_op jit(solution)/shard_map/dot_general | solution.py:75
  179.2 0.7 broadcast_in_dim.90
  179.9 6.9 %all-to-all-start.1 = ((f32[16,1,1024]{2,1,0:T(1,128)}), f32[16,1,1024]{2,1,0:T(1,128)S(1)}, u32[]{:S(2)}, u32[]{:S(2)}) async-start(f32[16,1,1024]{2,1,0:T(1,128)} %broadcast_in_dim.90), calls=%async_computation.1 | async-start | bytes 131072 | tf_op jit(solution)/shard_map/all_to_all | solution.py:17
  187.0 2.7 scatter_custom_fusion
  189.7 8.7 %all-to-all-done.1 = f32[16,1,1024]{2,1,0:T(1,128)S(1)} async-done(((f32[16,1,1024]{2,1,0:T(1,128)}), f32[16,1,1024]{2,1,0:T(1,128)S(1)}, u32[]{:S(2)}, u32[]{:S(2)}) %all-to-all-start.1) | async-done | bytes 65568 | tf_op jit(solution)/shard_map/all_to_all | solution.py:17
  198.5 4.4 %multiply_reduce_fusion = (f32[3200]{0:T(1024)S(1)}, f32[512,3200]{1,0:T(8,128)S(1)}) fusion(bf16[1,512,3200]{2,1,0:T(8,128)(2,1)} %all-gather.5.cloned.1.call-done, bf16[512,512]{0,1:T(8,128)(2,1)} %get-tuple-element.50, f32[512]{0:T(512)S(1)} %get-tuple-element.31, f32[512]{0:T(512)S(1)} %get-tuple-element.30, f32[512]{0:T(512)S(1)} %dynamic_slice.14, ...), kind=kOutput, calls=%fused_computation.12 | convolution fusion | flops 1683354496 | bytes 10898432 | tf_op jit(solution)/shard_map/dot_general | solution.py:123
  202.9 6.5 %fusion.6 = bf16[3200,512]{0,1:T(8,128)(2,1)} fusion(f32[512,3200]{1,0:T(8,128)S(1)} %get-tuple-element.52, f32[3200]{0:T(1024)S(1)} %convert_reduce_fusion.1, f32[512]{0:T(512)S(1)} %bitcast.103, f32[3200]{0:T(1024)S(1)} %reduce.13, f32[3200]{0:T(1024)S(1)} %add_sqrt_fusion), kind=kLoop, calls=%fused_computation.13 | loop fusion | flops 29491200 | bytes 9870848 | tf_op jit(solution)/shard_map/convert_element_type | solution.py:127
  209.5 1.4 dynamic-slice.1
  211.6 2.1 fusion.10
  213.7 2.5 fusion.9
  216.2 0.3 fusion.22
  216.4 0.2 add_dynamic-update-slice_fusion
  216.6 14.0 %psum.28 = f32[8192]{0:T(1024)S(1)} all-reduce(f32[8192]{0:T(1024)S(1)} %add_dynamic-update-slice_fusion), channel_id=1, replica_groups=mesh['dp_0'=4,'dp_1'=4,'dp_2'=2,'seq'=16] {'dp_0'}, use_global_device_ids=true, to_apply=%region_11.12 | all-reduce | flops 8192 | bytes 65536 | tf_op jit(solution)/shard_map/psum | solution.py:36
  230.7 14.3 %psum.29 = f32[8192]{0:T(1024)S(1)} all-reduce(f32[8192]{0:T(1024)S(1)} %psum.28), channel_id=1, replica_groups=mesh['dp_0'=4,'dp_1'=4,'dp_2'=2,'seq'=16] {'dp_1'}, use_global_device_ids=true, to_apply=%region_12.13 | all-reduce | flops 8192 | bytes 65536 | tf_op jit(solution)/shard_map/psum | solution.py:36
  244.9 18.2 %psum.30 = f32[8192]{0:T(1024)S(1)} all-reduce(f32[8192]{0:T(1024)S(1)} %psum.29), channel_id=1, replica_groups=mesh['dp_0'=4,'dp_1'=4,'dp_2'=2,'seq'=16] {'dp_2'}, use_global_device_ids=true, to_apply=%region_13.14 | all-reduce | flops 8192 | bytes 65536 | tf_op jit(solution)/shard_map/psum | solution.py:36
  263.1 41.1 %psum.31 = f32[8192]{0:T(1024)S(1)} all-reduce(f32[8192]{0:T(1024)S(1)} %psum.30), channel_id=1, replica_groups=mesh['dp_0'=4,'dp_1'=4,'dp_2'=2,'seq'=16] {'seq'}, use_global_device_ids=true, to_apply=%region_14.15 | all-reduce | flops 8192 | bytes 65536 | tf_op jit(solution)/shard_map/psum | solution.py:36
  304.2 0.6 broadcast_multiply_fusion
  304.8 45.4 %all-reduce.3.cloned.1.call-done = bf16[3200,512]{0,1:T(8,128)(2,1)} async-done(((bf16[3200,512]{0,1:T(8,128)(2,1)}), bf16[3200,512]{0,1:T(8,128)(2,1)}) %all-reduce.3.cloned.1.call-update) | async-done | bytes 3276816
  350.3 1.1 convert_multiply_fusion.7
  351.3 0.8 copy.42
  (39 shorter events, 0.9 us)
Async XLA Ops:
  7.2 144.3 %all-gather.7.cloned.1.call-start = ((), (), s32[]{:S(2)}) async-start(), calls=%async_computation.3 | async-start | bytes 3514368 | tf_op jit(solution)/shard_map/all_gather | solution.py:77
  7.9 166.4 %all-gather.5.cloned.1.call-start = ((), (), s32[]{:S(2)}) async-start(), calls=%async_computation.2 | async-start | bytes 3481600 | tf_op jit(solution)/shard_map/all_gather | solution.py:73
  26.4 65.6 %copy-start = (s32[1,512]{1,0:T(1,128)S(1)}, s32[1,512]{1,0:T(1,128)}, u32[]{:S(2)}) copy-start(s32[1,512]{1,0:T(1,128)} %param.14) | copy-start | bytes 6148
  75.4 56.3 %all-to-all-start = ((bf16[16,2,12288]{2,1,0:T(2,128)(2,1)}), bf16[16,2,12288]{2,1,0:T(2,128)(2,1)S(1)}, u32[]{:S(2)}, u32[]{:S(2)}) async-start(bf16[16,2,12288]{2,1,0:T(2,128)(2,1)} %reshape.481), calls=%async_computation | async-start | bytes 1572864 | tf_op jit(solution)/shard_map/all_to_all | solution.py:97
  174.3 12.6 %copy-start.5 = (f32[1,1,3200]{2,1,0:T(1,128)S(1)}, f32[1,1,3200]{2,1,0:T(1,128)}, u32[]{:S(2)}) copy-start(f32[1,1,3200]{2,1,0:T(1,128)} %param.16) | copy-start | bytes 38404
  174.3 15.3 %copy-start.4 = (s32[1,1,3200]{2,1,0:T(1,128)S(1)}, s32[1,1,3200]{2,1,0:T(1,128)}, u32[]{:S(2)}) copy-start(s32[1,1,3200]{2,1,0:T(1,128)} %param.15) | copy-start | bytes 38404
  179.9 18.5 %all-to-all-start.1 = ((f32[16,1,1024]{2,1,0:T(1,128)}), f32[16,1,1024]{2,1,0:T(1,128)S(1)}, u32[]{:S(2)}, u32[]{:S(2)}) async-start(f32[16,1,1024]{2,1,0:T(1,128)} %broadcast_in_dim.90), calls=%async_computation.1 | async-start | bytes 131072 | tf_op jit(solution)/shard_map/all_to_all | solution.py:17
  186.8 163.4 %all-reduce.3.cloned.1.call-start = ((), (), s32[]{:S(2)}) async-start(), calls=%async_computation.4 | async-start | bytes 6553600
  198.5 4.4 %copy-start.6 = (f32[1,512]{1,0:T(1,128)S(1)}, f32[1,512]{1,0:T(1,128)}, u32[]{:S(2)}) copy-start(f32[1,512]{1,0:T(1,128)} %param.17) | copy-start | bytes 6148
  209.4 4.3 %copy-start.1 = (bf16[1,128,8192]{2,1,0:T(8,128)(2,1)S(1)}, bf16[1,128,8192]{2,1,0:T(8,128)(2,1)}, u32[]{:S(2)}) copy-start(bf16[1,128,8192]{2,1,0:T(8,128)(2,1)} %param.12) | copy-start | bytes 6291460
  209.4 6.8 %copy-start.2 = (bf16[512,512]{0,1:T(8,128)(2,1)S(1)}, bf16[512,512]{0,1:T(8,128)(2,1)}, u32[]{:S(2)}) copy-start(bf16[512,512]{0,1:T(8,128)(2,1)} %copy.40) | copy-start | bytes 1572868
  209.4 6.8 %copy-start.3 = (bf16[512,512]{0,1:T(8,128)(2,1)S(1)}, bf16[512,512]{0,1:T(8,128)(2,1)}, u32[]{:S(2)}) copy-start(bf16[512,512]{0,1:T(8,128)(2,1)} %get-tuple-element.50) | copy-start | bytes 1572868
Sparse Core Ops, SparseCore 0:
  11.1 66.3 all-gather.6
  79.6 94.6 all-gather.4
  209.5 140.6 all-reduce.2
where the time goes:
time: 360 us; the launch traced here: 359 us
  waiting for transfers between devices  104 us (29%)
  blocking collectives  87.6 us (24%)
  other arithmetic  72.6 us (20%)
  local copies, waits for them, and re-layouts  47.6 us (13%)
  starting transfers between devices  22.8 us (6%)
  between operations  14.7 us (4%)
  matrix products  9.27 us (3%)
    psum x4, blocking collectives, one_axis_at_a_time(): value = lax.psum(value, axis)  87.6 us
    unnamed x4, waiting for transfers between devices  46.8 us
    unnamed x2, other arithmetic  45.2 us
    all_to_all x1, waiting for transfers between devices, on_device(): lax.all_to_all(outgoing[None], 'seq', split_axis=2, concat_axis=0, tiled=...  29.5 us
    all_gather x1, waiting for transfers between devices, on_device(): gathered = lax.all_gather(tile_tokens[0], 'seq', axis=0, tiled=True)  19.1 us
    unnamed x21, local copies, waits for them, and re-layouts  18.5 us
    all_to_all x1, starting transfers between devices, on_device(): lax.all_to_all(outgoing[None], 'seq', split_axis=2, concat_axis=0, tiled=...  15.8 us
    all_to_all x1, waiting for transfers between devices, copy_for_each(): return lax.all_to_all(copies, axis, split_axis=0, concat_axis=0, tiled=True)  8.72 us
  transfers between devices with their start and end apart: 5, of which 4 were waited for; matrix products, arithmetic and copies ran while one was open for 31% of the time, Pallas kernels for 0%

commit v1 on v0

v1 whole, which is shorter than its diff:
```python
import functools

import jax
import jax.numpy as jnp
from jax import lax
from jax.experimental import pallas as pl
from jax.experimental.pallas import tpu as pltpu
from jax.sharding import Mesh
from jax.sharding import PartitionSpec as P

DP = ("dp_0", "dp_1", "dp_2")
MESH = pl.DeviceIdType.MESH
EPSILON = 1e-06
SLOTS = 48
GROUP = 4
F32 = jnp.float32
BF16 = jnp.bfloat16


def up(n, m):
    return -(-n // m) * m


def dot(a, b, dims=((1,), (0,))):
    return lax.dot_general(a, b, (dims, ((), ())), preferred_element_type=F32)


def iota(shape, axis):
    return lax.broadcasted_iota(jnp.int32, shape, axis)


def one_where(condition):
    return jnp.where(condition, 1.0, 0.0).astype(BF16)


def kernel(
    sizes,
    tile, w_own, cot, gain, places, levels, row_draws, column_draws, text_hbm,
    out, gain_out,
    tbuf, t_t, wbuf, wfull, text, outb, inb, emb, eg, icot, picks, sm_c, smb, marks, gacc,
    gz, gz_in, g_core, g_x, g_y, meta, qq, from_core, s_a, s_b, r_a, r_b, t_a, t_b, u_a, u_b, fown, f_in,
    text_sem, ag_s, ag_r, wx_s, wx_r, wy_s, wy_r, wc_s, wc_r, a2a_s, a2a_r, sm_s, sm_r, gz_s, gz_r,
    gc_s, gc_r, gx_s, gx_r, gy_s, gy_r, gf_s, gf_r, qc_s, qc_r,
    xa_s, xa_r, ya_s, ya_r, yb_s, yb_r, xb_s, xb_r, f_s, f_r,
):
    nx, ny, nz = sizes
    rows = w_own.shape[0]
    own_rows = t_t.shape[0] // (nx * ny * 2)
    img_dev, vd = tile.shape
    half_rows = img_dev // 2
    img = tbuf.shape[0]
    tok, d = cot.shape
    cols = w_own.shape[1]
    win = qq.shape[2]
    hc = cols // 2
    qc = cols // 4
    h = nz // 2
    mx, my, mc, mz = (lax.axis_index(a) for a in ("dp_0", "dp_1", "dp_2", "seq"))
    oc = 1 - mc

    def z_peer(k):
        return {"seq": lax.rem(mz + k, nz)}

    def z_source(k):
        return lax.rem(mz + nz - k, nz)

    def x_peer(k):
        return lax.rem(mx + k, nx)

    def y_peer(k):
        return lax.rem(my + k, ny)

    def x_source(k):
        return lax.rem(mx + nx - k, nx)

    def y_source(k):
        return lax.rem(my + ny - k, ny)

    def remote(src, dst, send, recv, where):
        return pltpu.make_async_remote_copy(
            src_ref=src, dst_ref=dst, send_sem=send, recv_sem=recv, device_id=where, device_id_type=MESH
        )

    text_copy = pltpu.make_async_copy(text_hbm, text, text_sem)
    text_copy.start()

    barrier = pltpu.get_barrier_semaphore()

    def greet(where):
        pl.semaphore_signal(barrier, inc=1, device_id=where, device_id_type=MESH)

    def greet_z(k, c):
        greet(z_peer(k))
        return c

    lax.fori_loop(1, nz, greet_z, 0)
    for k in range(1, nx):
        greet({"dp_0": x_peer(k)})
    for k in range(1, ny):
        greet({"dp_1": y_peer(k)})
    greet({"dp_2": oc})

    tbuf[h * img_dev : (h + 1) * img_dev, :] = tile[...]
    wbuf[mx, my, mc] = w_own[...]
    base = mz * tok
    here = places[...]
    found = here == base + iota((tok, img), 0)
    marks[...] = jnp.broadcast_to(jnp.sum(jnp.where(found, 1.0, 0.0), axis=1, keepdims=True), marks.shape)
    start = jnp.sum(jnp.where(here < base, 1, 0), axis=1, keepdims=True)
    slot_of = one_where(iota((SLOTS, img), 1) - start == iota((SLOTS, img), 0))
    select = dot(slot_of, one_where(found), ((1,), (1,))).astype(BF16)

    pl.semaphore_wait(barrier, (nz - 1) + (nx - 1) + (ny - 1) + 1)

    def ring(flow, step, half):
        src_block = h - (step - 1) if flow == 0 else h + (step - 1)
        dst_block = (h - step if flow == 0 else h + step) % nz
        src = tbuf.at[pl.ds(src_block * img_dev + half * half_rows, half_rows)]
        dst = tbuf.at[pl.ds(dst_block * img_dev + half * half_rows, half_rows)]
        where = {"seq": lax.rem(mz + 1, nz) if flow == 0 else lax.rem(mz + nz - 1, nz)}
        return remote(src, dst, ag_s.at[flow, step, half], ag_r.at[flow, step, half], where)

    def in_ring(flow, step, half):
        return step < h or (step == h and half == flow)

    for half in range(2):
        for flow in range(2):
            if in_ring(flow, 1, half):
                ring(flow, 1, half).start()

    def ring_step(s):
        for half in range(2):
            for flow in range(2):
                if in_ring(flow, s, half):
                    ring(flow, s, half).wait_recv()
                    if in_ring(flow, s + 1, half):
                        ring(flow, s + 1, half).start()

    def w_x(k, slot):
        return remote(wbuf.at[slot, my, mc], wbuf.at[slot, my, mc], wx_s.at[k], wx_r.at[k], {"dp_0": x_peer(k)})

    def w_y(k, slot):
        return remote(wbuf.at[:, slot, mc], wbuf.at[:, slot, mc], wy_s.at[k], wy_r.at[k], {"dp_1": y_peer(k)})

    def w_core(slot):
        return remote(wbuf.at[:, :, slot], wbuf.at[:, :, slot], wc_s, wc_r, {"dp_2": oc})

    for k in range(1, nx):
        w_x(k, mx).start()

    def send_rows(k):
        to = lax.rem(mz + k, nz)
        return remote(
            outb.at[to], inb.at[pl.ds(pl.multiple_of(mz * SLOTS, 16), SLOTS)], a2a_s.at[k], a2a_r.at[k], z_peer(k)
        )

    def take_rows(k):
        return remote(
            outb.at[0], inb.at[pl.ds(pl.multiple_of(z_source(k) * SLOTS, 16), SLOTS)], a2a_s.at[k], a2a_r.at[k], z_peer(k)
        )

    def outgoing(z):
        at = pl.ds(pl.multiple_of(z * cols, 128), cols)
        return dot(select, cot[:, at]).astype(BF16)

    def pick(k, c):
        to = lax.rem(mz + k, nz)
        outb[to] = outgoing(to)
        send_rows(k).start()
        return c

    lax.fori_loop(1, nz, pick, 0)
    inb[pl.ds(pl.multiple_of(mz * SLOTS, 16), SLOTS), :] = outgoing(mz)

    text_copy.wait()
    gacc[...] = jnp.zeros_like(gacc)

    def text_rows(i, c):
        at = pl.ds(pl.multiple_of(i * 16, 16), 16)
        squares = jnp.zeros((16, 1), F32)
        for z in range(nz):
            t = text[at, z * cols : (z + 1) * cols].astype(F32)
            squares += jnp.sum(t * t, axis=1, keepdims=True)
        inverse = jnp.where(marks[at, :1] > 0.5, 0.0, lax.rsqrt(squares / d + EPSILON))
        for z in range(nz):
            span = slice(z * cols, (z + 1) * cols)
            term = cot[at, span].astype(F32) * text[at, span].astype(F32) * inverse
            gacc[:, span] += term[:8] + term[8:]
        return c

    def text_part(first, last):
        lax.fori_loop(first, last, text_rows, 0)

    def send_gz(k):
        return remote(gz.at[lax.rem(mz + k, nz)], gz_in.at[mz], gz_s.at[k], gz_r.at[k], z_peer(k))

    def take_gz(k):
        return remote(gz.at[0], gz_in.at[z_source(k)], gz_s.at[k], gz_r.at[k], z_peer(k))

    def send_text_gain():
        for z in range(nz):
            gz[z] = jnp.sum(gacc[:, z * cols : (z + 1) * cols], axis=0, keepdims=True)

        def go(k, c):
            send_gz(k).start()
            return c

        lax.fori_loop(1, nz, go, 0)
        gz_in[mz] = gz[mz]

    def token_picks():
        slots = nz * SLOTS
        at = iota((1, slots), 1).astype(F32)
        owner = jnp.floor((at + 0.5) * (1.0 / SLOTS))
        placed = jnp.transpose(jnp.broadcast_to(here.astype(F32), (128, img)))[:, :1]
        first = jnp.sum(jnp.where(placed < owner * tok, 1.0, 0.0), axis=0, keepdims=True)
        last = jnp.sum(jnp.where(placed < owner * tok + tok, 1.0, 0.0), axis=0, keepdims=True)
        wanted = first + (at - owner * SLOTS)
        wanted = jnp.where(wanted < last, wanted, -1.0)
        for block in range(nz):
            shard = lax.rem(mz + nz - h + block, nz)
            token = (shard * img_dev + iota((img_dev, 1), 0)).astype(F32)
            picks[block * img_dev : (block + 1) * img_dev, :] = one_where(token == wanted)

    def bucket_columns():
        for at in range(0, vd, 128):
            n = min(128, vd - at)
            s = levels[:, at : at + n].astype(F32)
            r = 0.5 * row_draws[:, at : at + n]
            row = iota((128, n), 0)
            meta[at : at + n, :] = jnp.transpose(jnp.where(row == 0, s, jnp.where(row == 1, r, 0.0)))

    def pack_projector():
        wide, packed = 4 * rows, 4 * own_rows
        i, j = iota((packed, wide), 0), iota((packed, wide), 1)
        shift = jnp.zeros((packed, wide), F32)
        for b in range(4):
            hit = (j - b * rows == i - b * own_rows) & (i >= b * own_rows) & (i < (b + 1) * own_rows)
            shift = jnp.where(hit, 1.0, shift)
        shift = shift.astype(BF16)

        def pack(g, c):
            x, y = g // (ny // 2), lax.rem(g, ny // 2) * 2
            block = wbuf[x, pl.ds(y, 2)].reshape(wide, cols)
            wfull[pl.ds(pl.multiple_of(g * packed, 16), packed), :] = dot(shift, block).astype(BF16)
            return c

        lax.fori_loop(0, nx * ny // 2, pack, 0)

    token_group = GROUP * img_dev

    def token_rows(g):
        at = slice(g * token_group, (g + 1) * token_group)
        emb[at, :] = dot(tbuf[at, :], wfull[...]).astype(BF16)

    def flip(g):
        at = slice(g * token_group, (g + 1) * token_group)
        for v in range(0, vd, 640):
            n = min(640, vd - v)
            t_t[v : v + n, at] = jnp.transpose(tbuf[at, v : v + n])

    groups = nz // GROUP
    done_at = [max(abs(GROUP * g - h), abs(GROUP * g + GROUP - 1 - h)) for g in range(groups)]

    plan = {s: [] for s in range(1, h + 1)}

    def at_step(s, job):
        plan[min(max(s, 1), h)].append(job)

    def w_second():
        for k in range(1, nx):
            w_x(k, x_source(k)).wait_recv()
        for k in range(1, ny):
            w_y(k, my).start()

    def w_third():
        for k in range(1, ny):
            w_y(k, y_source(k)).wait_recv()
        w_core(mc).start()

    def w_last():
        w_core(oc).wait_recv()
        pack_projector()

    row_chunks = tok // 16
    w_done = min(5, h)
    at_step(1, lambda: text_part(0, row_chunks // 2))
    at_step(1, w_second)
    at_step(2, lambda: text_part(row_chunks // 2, row_chunks))
    at_step(2, send_text_gain)
    at_step(3, w_third)
    at_step(3, bucket_columns)
    at_step(4, token_picks)
    at_step(w_done, w_last)
    for g in sorted(range(groups), key=lambda g: done_at[g]):
        at_step(max(done_at[g], w_done), functools.partial(token_rows, g))
        at_step(done_at[g], functools.partial(flip, g))

    for s in range(1, h + 1):
        ring_step(s)
        for job in plan[s]:
            job()

    def wait_rows(k, c):
        take_rows(k).wait_recv()
        return c

    lax.fori_loop(1, nz, wait_rows, 0)
    own_gain = gain[mz]

    def token_sums(g, c):
        at = pl.ds(pl.multiple_of(g * token_group, token_group), token_group)
        e = emb[at, :].astype(F32)
        ic = dot(picks[at, :], inb[...])
        icot[at, :] = ic
        squares = jnp.sum(e * e, axis=1, keepdims=True)
        mixed = jnp.sum(ic * own_gain * e, axis=1, keepdims=True)
        lane = iota((token_group, 128), 1)
        sm_c[at, :] = jnp.where(lane == 0, squares, jnp.where(lane == 1, mixed, 0.0))
        return c

    lax.fori_loop(0, groups, token_sums, 0)
    turn = img_dev * lax.rem(mz + nz - h, nz)
    turn_back = img_dev * lax.rem(h + nz - mz, nz)
    smb[mz] = pltpu.roll(jnp.transpose(sm_c[...])[:8], turn, 1)

    def send_sums(k, source):
        return remote(smb.at[source], smb.at[source], sm_s.at[k], sm_r.at[k], z_peer(k))

    def go_sums(k, c):
        send_sums(k, mz).start()
        return c

    def wait_sums(k, c):
        send_sums(k, z_source(k)).wait_recv()
        return c

    lax.fori_loop(1, nz, go_sums, 0)
    lax.fori_loop(1, nz, wait_sums, 0)
    total = smb[0]
    for z in range(1, nz):
        total = total + smb[z]
    total = pltpu.roll(total, turn_back, 1)
    inverse = lax.rsqrt(total[0:1] / d + EPSILON)
    factor = total[1:2] * inverse / d * inverse
    row = iota((128, img), 0)
    sm_c[...] = jnp.transpose(jnp.where(row == 0, inverse, jnp.where(row == 1, factor, 0.0)))

    def token_grads(g, part):
        at = pl.ds(pl.multiple_of(g * token_group, token_group), token_group)
        e = emb[at, :].astype(F32)
        ic = icot[at, :]
        inv, fac = sm_c[at, 0:1], sm_c[at, 1:2]
        eg[at, :] = ((ic * own_gain - e * fac) * inv).astype(BF16)
        return part + jnp.sum(ic * e * inv, axis=0, keepdims=True)

    part = lax.fori_loop(0, groups, token_grads, jnp.zeros((1, cols), F32))

    def wait_gz(k, c):
        take_gz(k).wait_recv()
        return c

    lax.fori_loop(1, nz, wait_gz, 0)
    for z in range(nz):
        part = part + gz_in[z]
    g_core[mc] = part

    def gain_core(slot):
        return remote(g_core.at[slot], g_core.at[slot], gc_s, gc_r, {"dp_2": oc})

    def gain_x(k, slot):
        return remote(g_x.at[slot], g_x.at[slot], gx_s.at[k], gx_r.at[k], {"dp_0": x_peer(k)})

    def gain_y(k, slot):
        return remote(g_y.at[slot], g_y.at[slot], gy_s.at[k], gy_r.at[k], {"dp_1": y_peer(k)})

    def gain_z(k, slot):
        return remote(gain_out.at[slot], gain_out.at[slot], gf_s.at[k], gf_r.at[k], z_peer(k))

    gain_core(mc).start()

    def gain_second():
        gain_core(oc).wait_recv()
        g_x[mx] = g_core[0] + g_core[1]
        for k in range(1, nx):
            gain_x(k, mx).start()

    def gain_third():
        for k in range(1, nx):
            gain_x(k, x_source(k)).wait_recv()
        so_far = g_x[0]
        for x in range(1, nx):
            so_far = so_far + g_x[x]
        g_y[my] = so_far
        for k in range(1, ny):
            gain_y(k, my).start()

    def gain_fourth():
        for k in range(1, ny):
            gain_y(k, y_source(k)).wait_recv()
        so_far = g_y[0]
        for y in range(1, ny):
            so_far = so_far + g_y[y]
        gain_out[mz] = so_far * (1.0 / (nx * ny * 2))

        def go(k, c):
            gain_z(k, mz).start()
            return c

        lax.fori_loop(1, nz, go, 0)

    column_part = 0.5 * column_draws[...]

    def window(q):
        at = pl.ds(pl.multiple_of(2 * own_rows * q - 8 * lax.rem(q, 2), 16), win)
        grad = dot(t_t[at, :], eg[...])
        norm = jnp.sqrt(jnp.sum(grad * grad, axis=1, keepdims=True) + EPSILON)
        s, r = meta[at, 0:1], meta[at, 1:2]
        ratio = jnp.abs(grad) * (s / norm)
        lower = jnp.floor(ratio)
        quantum = lower + jnp.clip(2.0 * (ratio - lower) - (r + column_part), 0.0, 1.0)
        size = quantum * (norm / s)
        value = jnp.where(grad < 0.0, -size, size).astype(BF16)
        qq[0, q] = value[:, :hc]
        qq[1, q] = value[:, hc:]

    def swap(k, x):
        at = pl.ds(x * ny, ny)
        return remote(qq.at[oc, at], from_core.at[at], qc_s.at[k], qc_r.at[k], {"dp_2": oc})

    def send_a(k):
        return remote(s_a.at[x_peer(k)], r_a.at[mx], xa_s.at[k], xa_r.at[k], {"dp_0": x_peer(k)})

    def take_a(k):
        return remote(s_a.at[0], r_a.at[x_source(k)], xa_s.at[k], xa_r.at[k], {"dp_0": x_peer(k)})

    def send_b(k):
        return remote(s_b.at[y_peer(k)], r_b.at[my], yb_s.at[k], yb_r.at[k], {"dp_1": y_peer(k)})

    def take_b(k):
        return remote(s_b.at[0], r_b.at[y_source(k)], yb_s.at[k], yb_r.at[k], {"dp_1": y_peer(k)})

    def x_at(k):
        return lax.rem(mx + k, nx)

    def windows(k):
        x = x_at(k)

        def one(y, c):
            window(x * ny + y)
            return c

        lax.fori_loop(0, ny, one, 0)
        swap(k, x).start()

    def sum_cores(k):
        x = x_at(k)
        swap(k, x).wait_recv()

        def one(y, c):
            both = (qq[mc, x * ny + y].astype(F32) + from_core[x * ny + y].astype(F32)).astype(BF16)
            s_a[x, y] = both[:, :qc]
            s_b[y, x] = both[:, qc:]
            return c

        lax.fori_loop(0, ny, one, 0)
        if k < nx:
            send_a(k).start()

    beside = [gain_second, gain_third, gain_fourth]
    for k in range(1, nx + 1):
        windows(k)
        if beside:
            beside.pop(0)()
        if k > 1:
            sum_cores(k - 1)
    sum_cores(nx)
    for k in range(1, ny):
        send_b(k).start()
    for job in beside:
        job()

    def send_a2(k):
        return remote(t_a.at[y_peer(k)], u_a.at[my], ya_s.at[k], ya_r.at[k], {"dp_1": y_peer(k)})

    def take_a2(k):
        return remote(t_a.at[0], u_a.at[y_source(k)], ya_s.at[k], ya_r.at[k], {"dp_1": y_peer(k)})

    def send_b2(k):
        return remote(t_b.at[x_peer(k)], u_b.at[mx], xb_s.at[k], xb_r.at[k], {"dp_0": x_peer(k)})

    def take_b2(k):
        return remote(t_b.at[0], u_b.at[x_source(k)], xb_s.at[k], xb_r.at[k], {"dp_0": x_peer(k)})

    for k in range(1, nx):
        take_a(k).wait_recv()

    def add_a(y, c):
        so_far = s_a[mx, y].astype(F32)
        for k in range(1, nx):
            so_far = so_far + r_a[x_source(k), y].astype(F32)
        t_a[y] = so_far.astype(BF16)
        return c

    lax.fori_loop(0, ny, add_a, 0)
    for k in range(1, ny):
        send_a2(k).start()
    for k in range(1, ny):
        take_b(k).wait_recv()

    def add_b(x, c):
        so_far = s_b[my, x].astype(F32)
        for k in range(1, ny):
            so_far = so_far + r_b[y_source(k), x].astype(F32)
        t_b[x] = so_far.astype(BF16)
        return c

    lax.fori_loop(0, nx, add_b, 0)
    for k in range(1, nx):
        send_b2(k).start()
    share = 1.0 / (nx * ny * 2)
    for k in range(1, ny):
        take_a2(k).wait_recv()
    so_far = t_a[my].astype(F32)
    for k in range(1, ny):
        so_far = so_far + u_a[y_source(k)].astype(F32)
    fown[:, :qc] = so_far * share
    for k in range(1, nx):
        take_b2(k).wait_recv()
    so_far = t_b[mx].astype(F32)
    for k in range(1, nx):
        so_far = so_far + u_b[x_source(k)].astype(F32)
    fown[:, qc:] = so_far * share

    step = win - rows

    def rows_of(core):
        return pl.ds(pl.multiple_of(core * step, 8), rows)

    last = remote(fown.at[rows_of(oc)], f_in, f_s, f_r, {"dp_2": oc})
    last.start()
    out[:, pl.ds(pl.multiple_of(mc * hc, 128), hc)] = fown[rows_of(mc), :]
    last.wait_recv()
    out[:, pl.ds(pl.multiple_of(oc * hc, 128), hc)] = f_in[...]

    def wait_gain(k, c):
        gain_z(k, z_source(k)).wait_recv()
        gain_z(k, mz).wait_send()
        send_rows(k).wait_send()
        send_gz(k).wait_send()
        send_sums(k, mz).wait_send()
        return c

    lax.fori_loop(1, nz, wait_gain, 0)
    for s in range(1, h + 1):
        for half in range(2):
            for flow in range(2):
                if in_ring(flow, s, half):
                    ring(flow, s, half).wait_send()
    for k in range(1, nx):
        w_x(k, mx).wait_send()
        gain_x(k, mx).wait_send()
        send_a(k).wait_send()
        send_b2(k).wait_send()
    for k in range(1, ny):
        w_y(k, my).wait_send()
        gain_y(k, my).wait_send()
        send_b(k).wait_send()
        send_a2(k).wait_send()
    w_core(mc).wait_send()
    gain_core(mc).wait_send()
    for k in range(1, nx + 1):
        swap(k, x_at(k)).wait_send()
    last.wait_send()


def on_device(
    sizes, tile_tokens, proj_weight, text_hidden, cotangent, norm_gain, placeholders, bucket_levels, row_draws, column_draws
):
    nx, ny, nz = sizes
    img_dev, vd = tile_tokens.shape[1:]
    own_rows, cols = proj_weight.shape
    tok, d = text_hidden.shape[1:]
    img = placeholders.shape[1]
    rows = up(own_rows, 16)
    win = up(2 * own_rows, 16)
    windows = nx * ny
    hc, qc = cols // 2, cols // 4
    h = nz // 2
    dma = pltpu.SemaphoreType.DMA
    vmem = pl.BlockSpec(memory_space=pltpu.VMEM)
    scratch = [
        pltpu.VMEM((img, vd), BF16),
        pltpu.VMEM((vd, img), BF16),
        pltpu.VMEM((nx, ny, 2, rows, cols), BF16),
        pltpu.VMEM((vd, cols), BF16),
        pltpu.VMEM((tok, d), BF16),
        pltpu.VMEM((nz, SLOTS, cols), BF16),
        pltpu.VMEM((nz * SLOTS, cols), BF16),
        pltpu.VMEM((img, cols), BF16),
        pltpu.VMEM((img, cols), BF16),
        pltpu.VMEM((img, cols), F32),
        pltpu.VMEM((img, nz * SLOTS), BF16),
        pltpu.VMEM((img, 128), F32),
        pltpu.VMEM((nz, 8, img), F32),
        pltpu.VMEM((tok, 128), F32),
        pltpu.VMEM((8, d), F32),
        pltpu.VMEM((nz, 1, cols), F32),
        pltpu.VMEM((nz, 1, cols), F32),
        pltpu.VMEM((2, 1, cols), F32),
        pltpu.VMEM((nx, 1, cols), F32),
        pltpu.VMEM((ny, 1, cols), F32),
        pltpu.VMEM((vd, 128), F32),
        pltpu.VMEM((2, windows, win, hc), BF16),
        pltpu.VMEM((windows, win, hc), BF16),
        pltpu.VMEM((nx, ny, win, qc), BF16),
        pltpu.VMEM((ny, nx, win, qc), BF16),
        pltpu.VMEM((nx, ny, win, qc), BF16),
        pltpu.VMEM((ny, nx, win, qc), BF16),
        pltpu.VMEM((ny, win, qc), BF16),
        pltpu.VMEM((nx, win, qc), BF16),
        pltpu.VMEM((ny, win, qc), BF16),
        pltpu.VMEM((nx, win, qc), BF16),
        pltpu.VMEM((win, hc), F32),
        pltpu.VMEM((rows, hc), F32),
        dma,
        dma((2, h + 1, 2)), dma((2, h + 1, 2)),
        dma((nx,)), dma((nx,)), dma((ny,)), dma((ny,)), dma, dma,
        dma((nz,)), dma((nz,)), dma((nz,)), dma((nz,)), dma((nz,)), dma((nz,)),
        dma, dma, dma((nx,)), dma((nx,)), dma((ny,)), dma((ny,)), dma((nz,)), dma((nz,)),
        dma((nx + 1,)), dma((nx + 1,)),
        dma((nx,)), dma((nx,)), dma((ny,)), dma((ny,)), dma((ny,)), dma((ny,)), dma((nx,)), dma((nx,)), dma, dma,
    ]
    summed, gain_total = pl.pallas_call(
        functools.partial(kernel, sizes),
        out_shape=(
            jax.ShapeDtypeStruct((rows, cols), F32),
            jax.ShapeDtypeStruct((nz, 1, cols), F32),
        ),
        in_specs=[vmem] * 8 + [pl.BlockSpec(memory_space=pl.ANY)],
        out_specs=(vmem, vmem),
        scratch_shapes=scratch,
        compiler_params=pltpu.CompilerParams(
            collective_id=0, has_side_effects=True, vmem_limit_bytes=56 * 2**20
        ),
    )(
        tile_tokens[0],
        jnp.pad(proj_weight, ((0, rows - own_rows), (0, 0))),
        cotangent[0],
        norm_gain.reshape(nz, 1, cols),
        placeholders,
        bucket_levels[0],
        row_draws[0],
        column_draws,
        text_hidden[0],
    )
    odd = (lax.axis_index("dp_0") * ny + lax.axis_index("dp_1")) % 2
    core = lax.axis_index("dp_2")
    at = odd * (win - 2 * own_rows) + core * (own_rows - (win - rows))
    return lax.dynamic_slice_in_dim(summed, at, own_rows, 0), gain_total.reshape(d)


def solution(mesh):
    nz = mesh.shape["seq"]
    nx, ny = (4, 4) if mesh.shape["dp"] == 32 else (2, mesh.shape["dp"] // 4)
    finer = Mesh(mesh.devices.reshape(nx, ny, 2, nz), (*DP, "seq"))
    return jax.shard_map(
        functools.partial(on_device, (nx, ny, nz)),
        mesh=finer,
        in_specs=(
            P(DP, "seq", None),
            P(DP, "seq"),
            P(DP, "seq", None),
            P(DP, "seq", None),
            P(),
            P(DP, None),
            P(DP, "seq", None),
            P(DP, "seq", None),
            P(DP, "seq"),
        ),
        out_specs=(P(DP, "seq"), P()),
        check_vma=False,
    )
```

time: 360 us -> 147 us (0.41)
  Pallas kernels: 0 us -> 142 us
  waiting for transfers between devices: 104 us -> 0 us
  blocking collectives: 87.6 us -> 0 us
  other arithmetic: 72.6 us -> 0 us
  local copies, waits for them, and re-layouts: 47.6 us -> 4.58 us
  starting transfers between devices: 22.8 us -> 0 us
  between operations: 14.7 us -> 0.66 us
  matrix products: 9.27 us -> 0 us
    pallas_call x0 -> x1, Pallas kernels: none -> 142 us  [on_device(): pl.pallas_call(functools.partial(kernel, sizes), out_shape=(jax.ShapeDtyp...]
    psum x4 -> x0, blocking collectives: 87.6 us -> none  [one_axis_at_a_time(): value = lax.psum(value, axis)]
    unnamed x4 -> x0, waiting for transfers between devices: 46.8 us -> none
    unnamed x2 -> x0, other arithmetic: 45.2 us -> none
    all_to_all x2 -> x0, waiting for transfers between devices: 38.2 us -> none  [the longest x1 29.5 us: on_device(): lax.all_to_all(outgoing[None], 'seq', split_axis=2, concat_axis=0, tiled=...]
    all_to_all x2 -> x0, starting transfers between devices: 22.7 us -> none  [the longest x1 15.8 us: on_device(): lax.all_to_all(outgoing[None], 'seq', split_axis=2, concat_axis=0, tiled=...]
    all_gather x2 -> x0, waiting for transfers between devices: 19.1 us -> none  [the longest x1 19.1 us: on_device(): gathered = lax.all_gather(tile_tokens[0], 'seq', axis=0, tiled=True)]
    unnamed x21 -> x1, local copies, waits for them, and re-layouts: 18.5 us -> 1.37 us
  transfers between devices with their start and end apart: 5 -> 0, of which waited for: 4 -> 0; matrix products, arithmetic and copies ran while one was open for 31% -> 0% of each run, Pallas kernels for 0% -> 0%
where the time goes in v1:
time: 147 us
  Pallas kernels  142 us (97%)
  local copies, waits for them, and re-layouts  4.58 us (3%)
    pallas_call x1, Pallas kernels, on_device(): pl.pallas_call(functools.partial(kernel, sizes), out_shape=(jax.ShapeDtyp...  142 us

profile of v1, /device:TPU:1, one launch (start us, length us, event | category | flops | bytes accessed | tf_op | source)
XLA Modules:
  0.0 147.1 jit_solution(9208543496218322260)
XLA Ops:
  0.6 1.6 %pad.4.w_own = bf16[112,512]{1,0:T(8,128)(2,1)} pad(bf16[100,512]{1,0:T(8,128)(2,1)} %param.10, bf16[]{:T(256)} %constant.26.clone.1), padding=0_12x0_0 | pad | bytes 217090 | tf_op jit(solution)/shard_map/jit(_pad)/pad | solution.py:648
  2.2 141.9 %shard_map.104 = (f32[112,512]{1,0:T(8,128)}, f32[16,1,512]{2,1,0:T(1,128)}) custom-call(bf16[32,3200]{1,0:T(8,128)(2,1)} %bitcast.9, bf16[112,512]{1,0:T(8,128)(2,1)} %pad.4.w_own, bf16[128,8192]{1,0:T(8,128)(2,1)} %bitcast.7, f32[16,1,512]{2,1,0:T(1,128)} %bitcast.10, s32[1,512]{1,0:T(1,128)} %places.1, s32[1,3200]{1,0:T(1,128)} %bitcast.12, ...), custom_call_target="tpu_custom_call" | custom-call | tf_op jit(solution)/shard_map/pallas_call | solution.py:634
  144.1 1.7 %constant_dynamic-slice_fusion = f32[100,512]{1,0:T(8,128)} fusion(f32[112,512]{1,0:T(8,128)} %get-tuple-element.4, s32[]{:T(128)S(6)} %select_n.11), kind=kLoop, calls=%fused_computation | loop fusion | bytes 409604 | tf_op jit(solution)/shard_map/dynamic_slice | solution.py:660
  145.7 1.4 copy.12

commit v2 on v1

--- a/solution.py
+++ b/solution.py
@@ -35,22 +35,21 @@
 
 def kernel(
     sizes,
-    tile, w_own, cot, gain, places, levels, row_draws, column_draws, text_hbm,
+    tile, w_own, gain, places, levels, row_draws, column_draws, cot_hbm, text_hbm,
     out, gain_out,
-    tbuf, t_t, wbuf, wfull, text, outb, inb, emb, eg, icot, picks, sm_c, smb, marks, gacc,
-    gz, gz_in, g_core, g_x, g_y, meta, qq, from_core, s_a, s_b, r_a, r_b, t_a, t_b, u_a, u_b, fown, f_in,
-    text_sem, ag_s, ag_r, wx_s, wx_r, wy_s, wy_r, wc_s, wc_r, a2a_s, a2a_r, sm_s, sm_r, gz_s, gz_r,
+    tbuf, t_t, wbuf, wfull, cot, text, outb, inb, emb, eg, icot, picks, sm_c, smb, marks, gacc,
+    gz, gz_in, g_core, g_x, g_y, meta, qq, from_core, s_a, s_b, r_a, r_b, t_a, t_b, u_a, u_b, fown, f_in, grads,
+    cot_sem, text_sem, ag_s, ag_r, wx_s, wx_r, wy_s, wy_r, wc_s, wc_r, a2a_s, a2a_r, sm_s, sm_r, gz_s, gz_r,
     gc_s, gc_r, gx_s, gx_r, gy_s, gy_r, gf_s, gf_r, qc_s, qc_r,
     xa_s, xa_r, ya_s, ya_r, yb_s, yb_r, xb_s, xb_r, f_s, f_r,
 ):
     nx, ny, nz = sizes
-    rows = w_own.shape[0]
-    own_rows = t_t.shape[0] // (nx * ny * 2)
+    own_rows, cols = w_own.shape
+    rows = wbuf.shape[3]
     img_dev, vd = tile.shape
     half_rows = img_dev // 2
     img = tbuf.shape[0]
     tok, d = cot.shape
-    cols = w_own.shape[1]
     win = qq.shape[2]
     hc = cols // 2
     qc = cols // 4
@@ -81,6 +80,8 @@
             src_ref=src, dst_ref=dst, send_sem=send, recv_sem=recv, device_id=where, device_id_type=MESH
         )
 
+    cot_copy = pltpu.make_async_copy(cot_hbm, cot, cot_sem)
+    cot_copy.start()
     text_copy = pltpu.make_async_copy(text_hbm, text, text_sem)
     text_copy.start()
 
@@ -101,7 +102,8 @@
     greet({"dp_2": oc})
 
     tbuf[h * img_dev : (h + 1) * img_dev, :] = tile[...]
-    wbuf[mx, my, mc] = w_own[...]
+    same = iota((rows, own_rows), 0) == iota((rows, own_rows), 1)
+    wbuf[mx, my, mc] = dot(one_where(same), w_own[...]).astype(BF16)
     base = mz * tok
     here = places[...]
     found = here == base + iota((tok, img), 0)
@@ -169,6 +171,7 @@
         send_rows(k).start()
         return c
 
+    cot_copy.wait()
     lax.fori_loop(1, nz, pick, 0)
     inb[pl.ds(pl.multiple_of(mz * SLOTS, 16), SLOTS), :] = outgoing(mz)
 
@@ -228,7 +231,7 @@
             s = levels[:, at : at + n].astype(F32)
             r = 0.5 * row_draws[:, at : at + n]
             row = iota((128, n), 0)
-            meta[at : at + n, :] = jnp.transpose(jnp.where(row == 0, s, jnp.where(row == 1, r, 0.0)))
+            meta[at : at + n, :] = jnp.transpose(jnp.where(row == 0, s, jnp.where(row == 1, r, 1.0 / s)))
 
     def pack_projector():
         wide, packed = 4 * rows, 4 * own_rows
@@ -251,7 +254,11 @@
 
     def token_rows(g):
         at = slice(g * token_group, (g + 1) * token_group)
-        emb[at, :] = dot(tbuf[at, :], wfull[...]).astype(BF16)
+        rounded = dot(tbuf[at, :], wfull[...]).astype(BF16)
+        emb[at, :] = rounded
+        e = rounded.astype(F32)
+        squares = jnp.sum(e * e, axis=1, keepdims=True)
+        sm_c[at, :] = jnp.where(iota((token_group, 128), 1) == 0, squares, 0.0)
 
     def flip(g):
         at = slice(g * token_group, (g + 1) * token_group)
@@ -309,20 +316,18 @@
     own_gain = gain[mz]
 
     def token_sums(g, c):
-        at = pl.ds(pl.multiple_of(g * token_group, token_group), token_group)
-        e = emb[at, :].astype(F32)
-        ic = dot(picks[at, :], inb[...])
-        icot[at, :] = ic
-        squares = jnp.sum(e * e, axis=1, keepdims=True)
-        mixed = jnp.sum(ic * own_gain * e, axis=1, keepdims=True)
-        lane = iota((token_group, 128), 1)
-        sm_c[at, :] = jnp.where(lane == 0, squares, jnp.where(lane == 1, mixed, 0.0))
+        first = pl.multiple_of(g * token_group, token_group)
+        icot[pl.ds(first, token_group), :] = dot(picks[pl.ds(first, token_group), :], inb[...])
+        for i in range(0, token_group, 16):
+            at = pl.ds(first + i, 16)
+            mixed = jnp.sum(icot[at, :] * own_gain * emb[at, :].astype(F32), axis=1, keepdims=True)
+            sm_c[at, :] = jnp.where(iota((16, 128), 1) == 1, mixed, sm_c[at, :])
         return c
 
     lax.fori_loop(0, groups, token_sums, 0)
     turn = img_dev * lax.rem(mz + nz - h, nz)
     turn_back = img_dev * lax.rem(h + nz - mz, nz)
-    smb[mz] = pltpu.roll(jnp.transpose(sm_c[...])[:8], turn, 1)
+    smb[mz] = pltpu.roll(jnp.transpose(sm_c[...])[:8], turn, 1)[:2]
 
     def send_sums(k, source):
         return remote(smb.at[source], smb.at[source], sm_s.at[k], sm_r.at[k], z_peer(k))
@@ -340,21 +345,26 @@
     total = smb[0]
     for z in range(1, nz):
         total = total + smb[z]
-    total = pltpu.roll(total, turn_back, 1)
+    total = pltpu.roll(jnp.concatenate([total] * 4, axis=0), turn_back, 1)
     inverse = lax.rsqrt(total[0:1] / d + EPSILON)
     factor = total[1:2] * inverse / d * inverse
     row = iota((128, img), 0)
     sm_c[...] = jnp.transpose(jnp.where(row == 0, inverse, jnp.where(row == 1, factor, 0.0)))
 
     def token_grads(g, part):
-        at = pl.ds(pl.multiple_of(g * token_group, token_group), token_group)
-        e = emb[at, :].astype(F32)
-        ic = icot[at, :]
-        inv, fac = sm_c[at, 0:1], sm_c[at, 1:2]
-        eg[at, :] = ((ic * own_gain - e * fac) * inv).astype(BF16)
-        return part + jnp.sum(ic * e * inv, axis=0, keepdims=True)
-
-    part = lax.fori_loop(0, groups, token_grads, jnp.zeros((1, cols), F32))
+        first = pl.multiple_of(g * token_group, token_group)
+        for i in range(0, token_group, 16):
+            at = pl.ds(first + i, 16)
+            e = emb[at, :].astype(F32)
+            ic = icot[at, :]
+            inv, fac = sm_c[at, 0:1], sm_c[at, 1:2]
+            eg[at, :] = ((ic * own_gain - e * fac) * inv).astype(BF16)
+            term = ic * e * inv
+            part = part + term[:8] + term[8:]
+        return part
+
+    part = lax.fori_loop(0, groups, token_grads, jnp.zeros((8, cols), F32))
+    part = jnp.sum(part, axis=0, keepdims=True)
 
     def wait_gz(k, c):
         take_gz(k).wait_recv()
@@ -411,18 +421,26 @@
 
     column_part = 0.5 * column_draws[...]
 
-    def window(q):
-        at = pl.ds(pl.multiple_of(2 * own_rows * q - 8 * lax.rem(q, 2), 16), win)
-        grad = dot(t_t[at, :], eg[...])
-        norm = jnp.sqrt(jnp.sum(grad * grad, axis=1, keepdims=True) + EPSILON)
-        s, r = meta[at, 0:1], meta[at, 1:2]
-        ratio = jnp.abs(grad) * (s / norm)
-        lower = jnp.floor(ratio)
-        quantum = lower + jnp.clip(2.0 * (ratio - lower) - (r + column_part), 0.0, 1.0)
-        size = quantum * (norm / s)
-        value = jnp.where(grad < 0.0, -size, size).astype(BF16)
-        qq[0, q] = value[:, :hc]
-        qq[1, q] = value[:, hc:]
+    def first_row(q):
+        return pl.multiple_of(2 * own_rows * q - 8 * lax.rem(q, 2), 8)
+
+    def window(q, slot):
+        grads[slot] = dot(t_t[pl.ds(pl.multiple_of(first_row(q), 16), win), :], eg[...])
+
+    def quantize(q, slot):
+        for i in range(0, win, 16):
+            grad = grads[slot, i : i + 16, :]
+            at = pl.ds(first_row(q) + i, 16)
+            square = jnp.sum(grad * grad, axis=1, keepdims=True) + EPSILON
+            root = lax.rsqrt(square)
+            s, r, s_inverse = meta[at, 0:1], meta[at, 1:2], meta[at, 2:3]
+            ratio = jnp.abs(grad) * (s * root)
+            lower = jnp.floor(ratio)
+            quantum = lower + jnp.clip(2.0 * (ratio - lower) - (r + column_part), 0.0, 1.0)
+            size = quantum * (square * root * s_inverse)
+            value = jnp.where(grad < 0.0, -size, size).astype(BF16)
+            qq[0, q, i : i + 16, :] = value[:, :hc]
+            qq[1, q, i : i + 16, :] = value[:, hc:]
 
     def swap(k, x):
         at = pl.ds(x * ny, ny)
@@ -434,11 +452,13 @@
     def take_a(k):
         return remote(s_a.at[0], r_a.at[x_source(k)], xa_s.at[k], xa_r.at[k], {"dp_0": x_peer(k)})
 
-    def send_b(k):
-        return remote(s_b.at[y_peer(k)], r_b.at[my], yb_s.at[k], yb_r.at[k], {"dp_1": y_peer(k)})
-
-    def take_b(k):
-        return remote(s_b.at[0], r_b.at[y_source(k)], yb_s.at[k], yb_r.at[k], {"dp_1": y_peer(k)})
+    def send_b(k, j):
+        x = x_at(k)
+        return remote(s_b.at[y_peer(j), x], r_b.at[my, x], yb_s.at[k, j], yb_r.at[k, j], {"dp_1": y_peer(j)})
+
+    def take_b(k, j):
+        x = x_at(k)
+        return remote(s_b.at[0, x], r_b.at[y_source(j), x], yb_s.at[k, j], yb_r.at[k, j], {"dp_1": y_peer(j)})
 
     def x_at(k):
         return lax.rem(mx + k, nx)
@@ -446,11 +466,15 @@
     def windows(k):
         x = x_at(k)
 
-        def one(y, c):
-            window(x * ny + y)
+        def two(pair, c):
+            q = x * ny + 2 * pair
+            window(q, 0)
+            window(q + 1, 1)
+            quantize(q, 0)
+            quantize(q + 1, 1)
             return c
 
-        lax.fori_loop(0, ny, one, 0)
+        lax.fori_loop(0, ny // 2, two, 0)
         swap(k, x).start()
 
     def sum_cores(k):
@@ -466,6 +490,45 @@
         lax.fori_loop(0, ny, one, 0)
         if k < nx:
             send_a(k).start()
+        for j in range(1, ny):
+            send_b(k, j).start()
+
+    def send_a2(k):
+        return remote(t_a.at[y_peer(k)], u_a.at[my], ya_s.at[k], ya_r.at[k], {"dp_1": y_peer(k)})
+
+    def take_a2(k):
+        return remote(t_a.at[0], u_a.at[y_source(k)], ya_s.at[k], ya_r.at[k], {"dp_1": y_peer(k)})
+
+    def send_b2(k):
+        return remote(t_b.at[x_peer(k)], u_b.at[mx], xb_s.at[k], xb_r.at[k], {"dp_0": x_peer(k)})
+
+    def take_b2(k):
+        return remote(t_b.at[0], u_b.at[x_source(k)], xb_s.at[k], xb_r.at[k], {"dp_0": x_peer(k)})
+
+    def sum_b(k):
+        x = x_at(k)
+        for j in range(1, ny):
+            take_b(k, j).wait_recv()
+        so_far = s_b[my, x].astype(F32)
+        for j in range(1, ny):
+            so_far = so_far + r_b[y_source(j), x].astype(F32)
+        t_b[x] = so_far.astype(BF16)
+        if k < nx:
+            send_b2(k).start()
+
+    def add_a(y, c):
+        so_far = s_a[mx, y].astype(F32)
+        for k in range(1, nx):
+            so_far = so_far + r_a[x_source(k), y].astype(F32)
+        t_a[y] = so_far.astype(BF16)
+        return c
+
+    def sum_a():
+        for k in range(1, nx):
+            take_a(k).wait_recv()
+        lax.fori_loop(0, ny, add_a, 0)
+        for k in range(1, ny):
+            send_a2(k).start()
 
     beside = [gain_second, gain_third, gain_fourth]
     for k in range(1, nx + 1):
@@ -474,50 +537,14 @@
             beside.pop(0)()
         if k > 1:
             sum_cores(k - 1)
+        if k > 2:
+            sum_b(k - 2)
     sum_cores(nx)
-    for k in range(1, ny):
-        send_b(k).start()
     for job in beside:
         job()
-
-    def send_a2(k):
-        return remote(t_a.at[y_peer(k)], u_a.at[my], ya_s.at[k], ya_r.at[k], {"dp_1": y_peer(k)})
-
-    def take_a2(k):
-        return remote(t_a.at[0], u_a.at[y_source(k)], ya_s.at[k], ya_r.at[k], {"dp_1": y_peer(k)})
-
-    def send_b2(k):
-        return remote(t_b.at[x_peer(k)], u_b.at[mx], xb_s.at[k], xb_r.at[k], {"dp_0": x_peer(k)})
-
-    def take_b2(k):
-        return remote(t_b.at[0], u_b.at[x_source(k)], xb_s.at[k], xb_r.at[k], {"dp_0": x_peer(k)})
-
-    for k in range(1, nx):
-        take_a(k).wait_recv()
-
-    def add_a(y, c):
-        so_far = s_a[mx, y].astype(F32)
-        for k in range(1, nx):
-            so_far = so_far + r_a[x_source(k), y].astype(F32)
-        t_a[y] = so_far.astype(BF16)
-        return c
-
-    lax.fori_loop(0, ny, add_a, 0)
-    for k in range(1, ny):
-        send_a2(k).start()
-    for k in range(1, ny):
-        take_b(k).wait_recv()
-
-    def add_b(x, c):
-        so_far = s_b[my, x].astype(F32)
-        for k in range(1, ny):
-            so_far = so_far + r_b[y_source(k), x].astype(F32)
-        t_b[x] = so_far.astype(BF16)
-        return c
-
-    lax.fori_loop(0, nx, add_b, 0)
-    for k in range(1, nx):
-        send_b2(k).start()
+    sum_b(nx - 1)
+    sum_a()
+    sum_b(nx)
     share = 1.0 / (nx * ny * 2)
     for k in range(1, ny):
         take_a2(k).wait_recv()
@@ -565,13 +592,22 @@
     for k in range(1, ny):
         w_y(k, my).wait_send()
         gain_y(k, my).wait_send()
-        send_b(k).wait_send()
         send_a2(k).wait_send()
     w_core(mc).wait_send()
     gain_core(mc).wait_send()
     for k in range(1, nx + 1):
         swap(k, x_at(k)).wait_send()
+        for j in range(1, ny):
+            send_b(k, j).wait_send()
     last.wait_send()
+
+
+def finish(ny, for_odd, for_core, summed, gain, weight_out, gain_out):
+    odd = lax.rem(lax.axis_index("dp_1"), 2)
+    at = odd * for_odd + lax.axis_index("dp_2") * for_core
+    rows = summed.shape[0]
+    weight_out[...] = pltpu.roll(summed[...], lax.rem(rows - at, rows), 0)[: weight_out.shape[0]]
+    gain_out[...] = gain[...]
 
 
 def on_device(
@@ -595,6 +631,7 @@
         pltpu.VMEM((nx, ny, 2, rows, cols), BF16),
         pltpu.VMEM((vd, cols), BF16),
         pltpu.VMEM((tok, d), BF16),
+        pltpu.VMEM((tok, d), BF16),
         pltpu.VMEM((nz, SLOTS, cols), BF16),
         pltpu.VMEM((nz * SLOTS, cols), BF16),
         pltpu.VMEM((img, cols), BF16),
@@ -602,7 +639,7 @@
         pltpu.VMEM((img, cols), F32),
         pltpu.VMEM((img, nz * SLOTS), BF16),
         pltpu.VMEM((img, 128), F32),
-        pltpu.VMEM((nz, 8, img), F32),
+        pltpu.VMEM((nz, 2, img), F32),
         pltpu.VMEM((tok, 128), F32),
         pltpu.VMEM((8, d), F32),
         pltpu.VMEM((nz, 1, cols), F32),
@@ -623,13 +660,14 @@
         pltpu.VMEM((nx, win, qc), BF16),
         pltpu.VMEM((win, hc), F32),
         pltpu.VMEM((rows, hc), F32),
-        dma,
+        pltpu.VMEM((2, win, cols), F32),
+        dma, dma,
         dma((2, h + 1, 2)), dma((2, h + 1, 2)),
         dma((nx,)), dma((nx,)), dma((ny,)), dma((ny,)), dma, dma,
         dma((nz,)), dma((nz,)), dma((nz,)), dma((nz,)), dma((nz,)), dma((nz,)),
         dma, dma, dma((nx,)), dma((nx,)), dma((ny,)), dma((ny,)), dma((nz,)), dma((nz,)),
         dma((nx + 1,)), dma((nx + 1,)),
-        dma((nx,)), dma((nx,)), dma((ny,)), dma((ny,)), dma((ny,)), dma((ny,)), dma((nx,)), dma((nx,)), dma, dma,
+        dma((nx,)), dma((nx,)), dma((ny,)), dma((ny,)), dma((nx + 1, ny)), dma((nx + 1, ny)), dma((nx,)), dma((nx,)), dma, dma,
     ]
     summed, gain_total = pl.pallas_call(
         functools.partial(kernel, sizes),
@@ -637,27 +675,33 @@
             jax.ShapeDtypeStruct((rows, cols), F32),
             jax.ShapeDtypeStruct((nz, 1, cols), F32),
         ),
-        in_specs=[vmem] * 8 + [pl.BlockSpec(memory_space=pl.ANY)],
+        in_specs=[vmem] * 7 + [pl.BlockSpec(memory_space=pl.ANY)] * 2,
         out_specs=(vmem, vmem),
         scratch_shapes=scratch,
         compiler_params=pltpu.CompilerParams(
-            collective_id=0, has_side_effects=True, vmem_limit_bytes=56 * 2**20
+            collective_id=0, has_side_effects=True, vmem_limit_bytes=58 * 2**20
         ),
     )(
         tile_tokens[0],
-        jnp.pad(proj_weight, ((0, rows - own_rows), (0, 0))),
-        cotangent[0],
+        proj_weight,
         norm_gain.reshape(nz, 1, cols),
         placeholders,
         bucket_levels[0],
         row_draws[0],
         column_draws,
+        cotangent[0],
         text_hidden[0],
     )
-    odd = (lax.axis_index("dp_0") * ny + lax.axis_index("dp_1")) % 2
-    core = lax.axis_index("dp_2")
-    at = odd * (win - 2 * own_rows) + core * (own_rows - (win - rows))
-    return lax.dynamic_slice_in_dim(summed, at, own_rows, 0), gain_total.reshape(d)
+    weight, gain_grad = pl.pallas_call(
+        functools.partial(finish, ny, win - 2 * own_rows, own_rows - (win - rows)),
+        out_shape=(
+            jax.ShapeDtypeStruct((own_rows, cols), F32),
+            jax.ShapeDtypeStruct((nz, 1, cols), F32),
+        ),
+        in_specs=[vmem, vmem],
+        out_specs=(vmem, vmem),
+    )(summed, gain_total)
+    return weight, gain_grad.reshape(d)
 
 
 def solution(mesh):

time: 147 us -> 135 us (0.918)
  Pallas kernels: 142 us -> 134 us
  local copies, waits for them, and re-layouts: 4.58 us -> 0 us
    pallas_call x1, Pallas kernels: 142 us -> 132 us  [on_device(): pl.pallas_call(functools.partial(kernel, sizes), out_shape=(jax.ShapeDtyp...]
    pallas_call x0 -> x1, Pallas kernels: none -> 1.7 us  [on_device(): pl.pallas_call(functools.partial(finish, ny, win - 2 * own_rows, own_rows...]
    dynamic_slice x1 -> x0, local copies, waits for them, and re-layouts: 1.66 us -> none  [on_device(): lax.dynamic_slice_in_dim(summed, at, own_rows, 0)]
    pad x1 -> x0, local copies, waits for them, and re-layouts: 1.55 us -> none  [on_device(): jnp.pad(proj_weight, ((0, rows - own_rows), (0, 0)))]
where the time goes in v2:
time: 135 us
  Pallas kernels  134 us (99%)
    pallas_call x1, Pallas kernels, on_device(): pl.pallas_call(functools.partial(kernel, sizes), out_shape=(jax.ShapeDtyp...  132 us

profile of v2, /device:TPU:1, one launch (start us, length us, event | category | flops | bytes accessed | tf_op | source)
XLA Modules:
  0.0 134.5 jit_solution(12669634148974086700)
XLA Ops:
  0.6 132.2 %shard_map.104 = (f32[112,512]{1,0:T(8,128)}, f32[16,1,512]{2,1,0:T(1,128)}) custom-call(bf16[32,3200]{1,0:T(8,128)(2,1)} %bitcast.9, bf16[100,512]{1,0:T(8,128)(2,1)} %w_own.1, f32[16,1,512]{2,1,0:T(1,128)} %bitcast.10, s32[1,512]{1,0:T(1,128)} %places.1, s32[1,3200]{1,0:T(1,128)} %bitcast.11, f32[1,3200]{1,0:T(1,128)} %bitcast.12, f32[1,512]{1,0:T(1,128)} %column_draws.1, ...), custom_call_target="tpu_custom_call" | custom-call | tf_op jit(solution)/shard_map/pallas_call | solution.py:672
  132.8 1.7 %shard_map.105 = (f32[100,512]{1,0:T(8,128)}, f32[16,1,512]{2,1,0:T(1,128)}) custom-call(f32[112,512]{1,0:T(8,128)} %get-tuple-element.6.summed, f32[16,1,512]{2,1,0:T(1,128)} %get-tuple-element.7.gain), custom_call_target="tpu_custom_call" | custom-call | tf_op jit(solution)/shard_map/pallas_call | solution.py:695

commit v3 on v2

--- a/solution.py
+++ b/solution.py
@@ -13,6 +13,8 @@
 EPSILON = 1e-06
 SLOTS = 48
 GROUP = 4
+ORDER = (8, 1, 15, 7, 9, 2, 14, 6, 10, 3, 13, 5, 11, 4, 12)
+ROWS_AT_STEP = (3, 2, 2, 2, 2, 2, 2, 0, 0)
 F32 = jnp.float32
 BF16 = jnp.bfloat16
 
@@ -38,10 +40,10 @@
     tile, w_own, gain, places, levels, row_draws, column_draws, cot_hbm, text_hbm,
     out, gain_out,
     tbuf, t_t, wbuf, wfull, cot, text, outb, inb, emb, eg, icot, picks, sm_c, smb, marks, gacc,
-    gz, gz_in, g_core, g_x, g_y, meta, qq, from_core, s_a, s_b, r_a, r_b, t_a, t_b, u_a, u_b, fown, f_in, grads,
+    gz, gz_in, g_core, g_x, g_y, meta, qq, from_core, s_a, s_b, r_a, r_b, t_a, t_b, u_a, u_b, grads,
     cot_sem, text_sem, ag_s, ag_r, wx_s, wx_r, wy_s, wy_r, wc_s, wc_r, a2a_s, a2a_r, sm_s, sm_r, gz_s, gz_r,
     gc_s, gc_r, gx_s, gx_r, gy_s, gy_r, gf_s, gf_r, qc_s, qc_r,
-    xa_s, xa_r, ya_s, ya_r, yb_s, yb_r, xb_s, xb_r, f_s, f_r,
+    xa_s, xa_r, ya_s, ya_r, yb_s, yb_r, xb_s, xb_r,
 ):
     nx, ny, nz = sizes
     own_rows, cols = w_own.shape
@@ -50,9 +52,8 @@
     half_rows = img_dev // 2
     img = tbuf.shape[0]
     tok, d = cot.shape
-    win = qq.shape[2]
+    win = qq.shape[1]
     hc = cols // 2
-    qc = cols // 4
     h = nz // 2
     mx, my, mc, mz = (lax.axis_index(a) for a in ("dp_0", "dp_1", "dp_2", "seq"))
     oc = 1 - mc
@@ -165,14 +166,21 @@
         at = pl.ds(pl.multiple_of(z * cols, 128), cols)
         return dot(select, cot[:, at]).astype(BF16)
 
-    def pick(k, c):
+    def pick(k):
         to = lax.rem(mz + k, nz)
         outb[to] = outgoing(to)
         send_rows(k).start()
-        return c
+
+    order = list(ORDER) if nz == 16 else list(range(1, nz))
+
+    def pick_some(step):
+        amount = ROWS_AT_STEP[step] if nz == 16 else nz
+        for k in order[:amount]:
+            pick(k)
+        del order[:amount]
 
     cot_copy.wait()
-    lax.fori_loop(1, nz, pick, 0)
+    pick_some(0)
     inb[pl.ds(pl.multiple_of(mz * SLOTS, 16), SLOTS), :] = outgoing(mz)
 
     text_copy.wait()
@@ -305,6 +313,8 @@
 
     for s in range(1, h + 1):
         ring_step(s)
+        if order:
+            pick_some(s)
         for job in plan[s]:
             job()
 
@@ -439,12 +449,14 @@
             quantum = lower + jnp.clip(2.0 * (ratio - lower) - (r + column_part), 0.0, 1.0)
             size = quantum * (square * root * s_inverse)
             value = jnp.where(grad < 0.0, -size, size).astype(BF16)
-            qq[0, q, i : i + 16, :] = value[:, :hc]
-            qq[1, q, i : i + 16, :] = value[:, hc:]
+            qq[q, i : i + 16, :] = value
+
+    def rows_of(core):
+        return pl.ds(pl.multiple_of(core * (win - rows), 16), rows)
 
     def swap(k, x):
         at = pl.ds(x * ny, ny)
-        return remote(qq.at[oc, at], from_core.at[at], qc_s.at[k], qc_r.at[k], {"dp_2": oc})
+        return remote(qq.at[at, rows_of(oc)], from_core.at[at], qc_s.at[k], qc_r.at[k], {"dp_2": oc})
 
     def send_a(k):
         return remote(s_a.at[x_peer(k)], r_a.at[mx], xa_s.at[k], xa_r.at[k], {"dp_0": x_peer(k)})
@@ -482,9 +494,10 @@
         swap(k, x).wait_recv()
 
         def one(y, c):
-            both = (qq[mc, x * ny + y].astype(F32) + from_core[x * ny + y].astype(F32)).astype(BF16)
-            s_a[x, y] = both[:, :qc]
-            s_b[y, x] = both[:, qc:]
+            q = x * ny + y
+            both = (qq[q, rows_of(mc), :].astype(F32) + from_core[q].astype(F32)).astype(BF16)
+            s_a[x, y] = both[:, :hc]
+            s_b[y, x] = both[:, hc:]
             return c
 
         lax.fori_loop(0, ny, one, 0)
@@ -551,31 +564,20 @@
     so_far = t_a[my].astype(F32)
     for k in range(1, ny):
         so_far = so_far + u_a[y_source(k)].astype(F32)
-    fown[:, :qc] = so_far * share
+    out[:, :hc] = so_far * share
     for k in range(1, nx):
         take_b2(k).wait_recv()
     so_far = t_b[mx].astype(F32)
     for k in range(1, nx):
         so_far = so_far + u_b[x_source(k)].astype(F32)
-    fown[:, qc:] = so_far * share
-
-    step = win - rows
-
-    def rows_of(core):
-        return pl.ds(pl.multiple_of(core * step, 8), rows)
-
-    last = remote(fown.at[rows_of(oc)], f_in, f_s, f_r, {"dp_2": oc})
-    last.start()
-    out[:, pl.ds(pl.multiple_of(mc * hc, 128), hc)] = fown[rows_of(mc), :]
-    last.wait_recv()
-    out[:, pl.ds(pl.multiple_of(oc * hc, 128), hc)] = f_in[...]
+    out[:, hc:] = so_far * share
 
     def wait_gain(k, c):
         gain_z(k, z_source(k)).wait_recv()
         gain_z(k, mz).wait_send()
         send_rows(k).wait_send()
+        send_sums(k, mz).wait_send()
         send_gz(k).wait_send()
-        send_sums(k, mz).wait_send()
         return c
 
     lax.fori_loop(1, nz, wait_gain, 0)
@@ -599,7 +601,6 @@
         swap(k, x_at(k)).wait_send()
         for j in range(1, ny):
             send_b(k, j).wait_send()
-    last.wait_send()
 
 
 def finish(ny, for_odd, for_core, summed, gain, weight_out, gain_out):
@@ -621,7 +622,7 @@
     rows = up(own_rows, 16)
     win = up(2 * own_rows, 16)
     windows = nx * ny
-    hc, qc = cols // 2, cols // 4
+    hc = cols // 2
     h = nz // 2
     dma = pltpu.SemaphoreType.DMA
     vmem = pl.BlockSpec(memory_space=pltpu.VMEM)
@@ -648,18 +649,16 @@
         pltpu.VMEM((nx, 1, cols), F32),
         pltpu.VMEM((ny, 1, cols), F32),
         pltpu.VMEM((vd, 128), F32),
-        pltpu.VMEM((2, windows, win, hc), BF16),
-        pltpu.VMEM((windows, win, hc), BF16),
-        pltpu.VMEM((nx, ny, win, qc), BF16),
-        pltpu.VMEM((ny, nx, win, qc), BF16),
-        pltpu.VMEM((nx, ny, win, qc), BF16),
-        pltpu.VMEM((ny, nx, win, qc), BF16),
-        pltpu.VMEM((ny, win, qc), BF16),
-        pltpu.VMEM((nx, win, qc), BF16),
-        pltpu.VMEM((ny, win, qc), BF16),
-        pltpu.VMEM((nx, win, qc), BF16),
-        pltpu.VMEM((win, hc), F32),
-        pltpu.VMEM((rows, hc), F32),
+        pltpu.VMEM((windows, win, cols), BF16),
+        pltpu.VMEM((windows, rows, cols), BF16),
+        pltpu.VMEM((nx, ny, rows, hc), BF16),
+        pltpu.VMEM((ny, nx, rows, hc), BF16),
+        pltpu.VMEM((nx, ny, rows, hc), BF16),
+        pltpu.VMEM((ny, nx, rows, hc), BF16),
+        pltpu.VMEM((ny, rows, hc), BF16),
+        pltpu.VMEM((nx, rows, hc), BF16),
+        pltpu.VMEM((ny, rows, hc), BF16),
+        pltpu.VMEM((nx, rows, hc), BF16),
         pltpu.VMEM((2, win, cols), F32),
         dma, dma,
         dma((2, h + 1, 2)), dma((2, h + 1, 2)),
@@ -667,7 +666,7 @@
         dma((nz,)), dma((nz,)), dma((nz,)), dma((nz,)), dma((nz,)), dma((nz,)),
         dma, dma, dma((nx,)), dma((nx,)), dma((ny,)), dma((ny,)), dma((nz,)), dma((nz,)),
         dma((nx + 1,)), dma((nx + 1,)),
-        dma((nx,)), dma((nx,)), dma((ny,)), dma((ny,)), dma((nx + 1, ny)), dma((nx + 1, ny)), dma((nx,)), dma((nx,)), dma, dma,
+        dma((nx,)), dma((nx,)), dma((ny,)), dma((ny,)), dma((nx + 1, ny)), dma((nx + 1, ny)), dma((nx,)), dma((nx,)),
     ]
     summed, gain_total = pl.pallas_call(
         functools.partial(kernel, sizes),

time: 135 us -> 129 us (0.956); the launches traced: 135 us -> 127 us
  Pallas kernels: 134 us -> 126 us
    pallas_call x1, Pallas kernels: 132 us -> 124 us  [on_device(): pl.pallas_call(functools.partial(kernel, sizes), out_shape=(jax.ShapeDtyp...]
where the time goes in v3:
time: 129 us; the launch traced here: 127 us
  Pallas kernels  126 us (98%)
    pallas_call x1, Pallas kernels, on_device(): pl.pallas_call(functools.partial(kernel, sizes), out_shape=(jax.ShapeDtyp...  124 us

profile of v3, /device:TPU:1, one launch (start us, length us, event | category | flops | bytes accessed | tf_op | source)
XLA Modules:
  0.0 126.8 jit_solution(14408606458494918422)
XLA Ops:
  0.6 124.5 %shard_map.104 = (f32[112,512]{1,0:T(8,128)}, f32[16,1,512]{2,1,0:T(1,128)}) custom-call(bf16[32,3200]{1,0:T(8,128)(2,1)} %bitcast.9, bf16[100,512]{1,0:T(8,128)(2,1)} %w_own.1, f32[16,1,512]{2,1,0:T(1,128)} %bitcast.10, s32[1,512]{1,0:T(1,128)} %places.1, s32[1,3200]{1,0:T(1,128)} %bitcast.11, f32[1,3200]{1,0:T(1,128)} %bitcast.12, f32[1,512]{1,0:T(1,128)} %column_draws.1, ...), custom_call_target="tpu_custom_call" | custom-call | tf_op jit(solution)/shard_map/pallas_call | solution.py:671
  125.1 1.7 %shard_map.105 = (f32[100,512]{1,0:T(8,128)}, f32[16,1,512]{2,1,0:T(1,128)}) custom-call(f32[112,512]{1,0:T(8,128)} %get-tuple-element.6.summed, f32[16,1,512]{2,1,0:T(1,128)} %get-tuple-element.7.gain), custom_call_target="tpu_custom_call" | custom-call | tf_op jit(solution)/shard_map/pallas_call | solution.py:694

commit v4 on v3

--- a/solution.py
+++ b/solution.py
@@ -305,36 +305,52 @@
     at_step(2, send_text_gain)
     at_step(3, w_third)
     at_step(3, bucket_columns)
-    at_step(4, token_picks)
+    at_step(min(4, h - 1), token_picks)
     at_step(w_done, w_last)
     for g in sorted(range(groups), key=lambda g: done_at[g]):
         at_step(max(done_at[g], w_done), functools.partial(token_rows, g))
-        at_step(done_at[g], functools.partial(flip, g))
-
+        if done_at[g] < h - 1:
+            at_step(done_at[g], functools.partial(flip, g))
+
+    def wait_rows(k, c):
+        take_rows(k).wait_recv()
+        return c
+
+    own_gain = gain[mz]
+
+    def pick_group(g, c):
+        at = pl.ds(pl.multiple_of(g * token_group, token_group), token_group)
+        icot[at, :] = dot(picks[at, :], inb[...])
+        return c
+
+    def pick_arrived():
+        lax.fori_loop(1, nz, wait_rows, 0)
+        lax.fori_loop(0, groups, pick_group, 0)
+
+    def token_products(g):
+        def some(i, c):
+            at = pl.ds(pl.multiple_of(g * token_group + i * 32, 32), 32)
+            mixed = jnp.sum(icot[at, :] * own_gain * emb[at, :].astype(F32), axis=1, keepdims=True)
+            sm_c[at, :] = jnp.where(iota((32, 128), 1) == 1, mixed, sm_c[at, :])
+            return c
+
+        lax.fori_loop(0, token_group // 32, some, 0, unroll=True)
+
+    early = [g for g in range(groups) if done_at[g] < h]
+    late = [g for g in range(groups) if done_at[g] >= h]
     for s in range(1, h + 1):
+        if s == h and not order:
+            pick_arrived()
+            for g in early:
+                token_products(g)
         ring_step(s)
         if order:
             pick_some(s)
         for job in plan[s]:
             job()
-
-    def wait_rows(k, c):
-        take_rows(k).wait_recv()
-        return c
-
-    lax.fori_loop(1, nz, wait_rows, 0)
-    own_gain = gain[mz]
-
-    def token_sums(g, c):
-        first = pl.multiple_of(g * token_group, token_group)
-        icot[pl.ds(first, token_group), :] = dot(picks[pl.ds(first, token_group), :], inb[...])
-        for i in range(0, token_group, 16):
-            at = pl.ds(first + i, 16)
-            mixed = jnp.sum(icot[at, :] * own_gain * emb[at, :].astype(F32), axis=1, keepdims=True)
-            sm_c[at, :] = jnp.where(iota((16, 128), 1) == 1, mixed, sm_c[at, :])
-        return c
-
-    lax.fori_loop(0, groups, token_sums, 0)
+    for g in late:
+        token_products(g)
+
     turn = img_dev * lax.rem(mz + nz - h, nz)
     turn_back = img_dev * lax.rem(h + nz - mz, nz)
     smb[mz] = pltpu.roll(jnp.transpose(sm_c[...])[:8], turn, 1)[:2]
@@ -342,15 +358,23 @@
     def send_sums(k, source):
         return remote(smb.at[source], smb.at[source], sm_s.at[k], sm_r.at[k], z_peer(k))
 
-    def go_sums(k, c):
-        send_sums(k, mz).start()
+    def wait_gz(k, c):
+        take_gz(k).wait_recv()
         return c
 
     def wait_sums(k, c):
         send_sums(k, z_source(k)).wait_recv()
         return c
 
-    lax.fori_loop(1, nz, go_sums, 0)
+    for k in sorted(range(1, nz), key=lambda k: -min(k, nz - k)):
+        send_sums(k, mz).start()
+    for g in range(groups):
+        if done_at[g] >= h - 1:
+            flip(g)
+    lax.fori_loop(1, nz, wait_gz, 0)
+    text_gain = gz_in[0]
+    for z in range(1, nz):
+        text_gain = text_gain + gz_in[z]
     lax.fori_loop(1, nz, wait_sums, 0)
     total = smb[0]
     for z in range(1, nz):
@@ -376,14 +400,7 @@
     part = lax.fori_loop(0, groups, token_grads, jnp.zeros((8, cols), F32))
     part = jnp.sum(part, axis=0, keepdims=True)
 
-    def wait_gz(k, c):
-        take_gz(k).wait_recv()
-        return c
-
-    lax.fori_loop(1, nz, wait_gz, 0)
-    for z in range(nz):
-        part = part + gz_in[z]
-    g_core[mc] = part
+    g_core[mc] = part + text_gain
 
     def gain_core(slot):
         return remote(g_core.at[slot], g_core.at[slot], gc_s, gc_r, {"dp_2": oc})
@@ -454,15 +471,20 @@
     def rows_of(core):
         return pl.ds(pl.multiple_of(core * (win - rows), 16), rows)
 
-    def swap(k, x):
-        at = pl.ds(x * ny, ny)
-        return remote(qq.at[at, rows_of(oc)], from_core.at[at], qc_s.at[k], qc_r.at[k], {"dp_2": oc})
-
-    def send_a(k):
-        return remote(s_a.at[x_peer(k)], r_a.at[mx], xa_s.at[k], xa_r.at[k], {"dp_0": x_peer(k)})
-
-    def take_a(k):
-        return remote(s_a.at[0], r_a.at[x_source(k)], xa_s.at[k], xa_r.at[k], {"dp_0": x_peer(k)})
+    def y_at(j):
+        return lax.rem(my + j, ny)
+
+    def swap(k, j):
+        q = x_at(k) * ny + y_at(j)
+        return remote(qq.at[q, rows_of(oc)], from_core.at[q], qc_s.at[k, j], qc_r.at[k, j], {"dp_2": oc})
+
+    def send_a(k, j):
+        y = y_at(j)
+        return remote(s_a.at[x_at(k), y], r_a.at[mx, y], xa_s.at[k, j], xa_r.at[k, j], {"dp_0": x_peer(k)})
+
+    def take_a(k, j):
+        y = y_at(j)
+        return remote(s_a.at[0, y], r_a.at[x_source(k), y], xa_s.at[k, j], xa_r.at[k, j], {"dp_0": x_peer(k)})
 
     def send_b(k, j):
         x = x_at(k)
@@ -475,35 +497,20 @@
     def x_at(k):
         return lax.rem(mx + k, nx)
 
-    def windows(k):
-        x = x_at(k)
-
-        def two(pair, c):
-            q = x * ny + 2 * pair
-            window(q, 0)
-            window(q + 1, 1)
-            quantize(q, 0)
-            quantize(q + 1, 1)
-            return c
-
-        lax.fori_loop(0, ny // 2, two, 0)
-        swap(k, x).start()
-
-    def sum_cores(k):
-        x = x_at(k)
-        swap(k, x).wait_recv()
-
-        def one(y, c):
-            q = x * ny + y
-            both = (qq[q, rows_of(mc), :].astype(F32) + from_core[q].astype(F32)).astype(BF16)
-            s_a[x, y] = both[:, :hc]
-            s_b[y, x] = both[:, hc:]
-            return c
-
-        lax.fori_loop(0, ny, one, 0)
-        if k < nx:
-            send_a(k).start()
-        for j in range(1, ny):
+    def sum_cores(k, j):
+        x, y = x_at(k), y_at(j)
+        q = x * ny + y
+        swap(k, j).wait_recv()
+        both = (qq[q, rows_of(mc), :].astype(F32) + from_core[q].astype(F32)).astype(BF16)
+        s_a[x, y] = both[:, :hc]
+        s_b[y, x] = both[:, hc:]
+
+        @pl.when(k < nx)
+        def to_x():
+            send_a(k, j).start()
+
+        @pl.when(j < ny)
+        def to_y():
             send_b(k, j).start()
 
     def send_a2(k):
@@ -526,37 +533,58 @@
         for j in range(1, ny):
             so_far = so_far + r_b[y_source(j), x].astype(F32)
         t_b[x] = so_far.astype(BF16)
-        if k < nx:
-            send_b2(k).start()
-
-    def add_a(y, c):
+
+    def sum_a(j):
+        y = y_at(j)
+        for k in range(1, nx):
+            take_a(k, j).wait_recv()
         so_far = s_a[mx, y].astype(F32)
         for k in range(1, nx):
             so_far = so_far + r_a[x_source(k), y].astype(F32)
         t_a[y] = so_far.astype(BF16)
+
+    pairs = ny // 2
+    steps = nx * pairs
+    beside = {1: gain_second, 2: gain_third, 3: gain_fourth}
+
+    def pair_of(t):
+        return 1 + t // pairs, 2 * lax.rem(t, pairs) + 1
+
+    def step_pair(t, c):
+        k, j = pair_of(t)
+        base_q = x_at(k) * ny
+        window(base_q + y_at(j), 0)
+        window(base_q + y_at(j + 1), 1)
+        quantize(base_q + y_at(j), 0)
+        swap(k, j).start()
+        quantize(base_q + y_at(j + 1), 1)
+        swap(k, j + 1).start()
+        for at, job in beside.items():
+            pl.when(t == at * pairs - 1)(job)
+
+        @pl.when(t > 0)
+        def before():
+            k_last, j_last = pair_of(t - 1)
+            sum_cores(k_last, j_last)
+            sum_cores(k_last, j_last + 1)
+
+        @pl.when((t >= 3 * pairs - 1) & (lax.rem(t, pairs) == pairs - 1))
+        def second():
+            sum_b(k - 2)
+            send_b2(k - 2).start()
+
         return c
 
-    def sum_a():
-        for k in range(1, nx):
-            take_a(k).wait_recv()
-        lax.fori_loop(0, ny, add_a, 0)
-        for k in range(1, ny):
-            send_a2(k).start()
-
-    beside = [gain_second, gain_third, gain_fourth]
-    for k in range(1, nx + 1):
-        windows(k)
-        if beside:
-            beside.pop(0)()
-        if k > 1:
-            sum_cores(k - 1)
-        if k > 2:
-            sum_b(k - 2)
-    sum_cores(nx)
-    for job in beside:
-        job()
+    lax.fori_loop(0, steps, step_pair, 0)
+    sum_cores(nx, ny - 1)
+    sum_cores(nx, ny)
     sum_b(nx - 1)
-    sum_a()
+    if nx > 1:
+        send_b2(nx - 1).start()
+    for j in range(1, ny + 1):
+        sum_a(j)
+        if j < ny:
+            send_a2(j).start()
     sum_b(nx)
     share = 1.0 / (nx * ny * 2)
     for k in range(1, ny):
@@ -589,7 +617,8 @@
     for k in range(1, nx):
         w_x(k, mx).wait_send()
         gain_x(k, mx).wait_send()
-        send_a(k).wait_send()
+        for j in range(1, ny + 1):
+            send_a(k, j).wait_send()
         send_b2(k).wait_send()
     for k in range(1, ny):
         w_y(k, my).wait_send()
@@ -598,7 +627,8 @@
     w_core(mc).wait_send()
     gain_core(mc).wait_send()
     for k in range(1, nx + 1):
-        swap(k, x_at(k)).wait_send()
+        for j in range(1, ny + 1):
+            swap(k, j).wait_send()
         for j in range(1, ny):
             send_b(k, j).wait_send()
 
@@ -665,8 +695,8 @@
         dma((nx,)), dma((nx,)), dma((ny,)), dma((ny,)), dma, dma,
         dma((nz,)), dma((nz,)), dma((nz,)), dma((nz,)), dma((nz,)), dma((nz,)),
         dma, dma, dma((nx,)), dma((nx,)), dma((ny,)), dma((ny,)), dma((nz,)), dma((nz,)),
-        dma((nx + 1,)), dma((nx + 1,)),
-        dma((nx,)), dma((nx,)), dma((ny,)), dma((ny,)), dma((nx + 1, ny)), dma((nx + 1, ny)), dma((nx,)), dma((nx,)),
+        dma((nx + 1, ny + 1)), dma((nx + 1, ny + 1)),
+        dma((nx, ny + 1)), dma((nx, ny + 1)), dma((ny,)), dma((ny,)), dma((nx + 1, ny)), dma((nx + 1, ny)), dma((nx,)), dma((nx,)),
     ]
     summed, gain_total = pl.pallas_call(
         functools.partial(kernel, sizes),

time: 129 us -> 123 us (0.953)
  Pallas kernels: 126 us -> 121 us
    pallas_call x1, Pallas kernels: 124 us -> 120 us  [on_device(): pl.pallas_call(functools.partial(kernel, sizes), out_shape=(jax.ShapeDtyp...]
where the time goes in v4:
time: 123 us; the launch traced here: 122 us
  Pallas kernels  121 us (98%)
    pallas_call x1, Pallas kernels, on_device(): pl.pallas_call(functools.partial(kernel, sizes), out_shape=(jax.ShapeDtyp...  120 us

profile of v4, /device:TPU:1, one launch (start us, length us, event | category | flops | bytes accessed | tf_op | source)
XLA Modules:
  0.0 122.1 jit_solution(16346883505075189892)
XLA Ops:
  0.6 119.7 %shard_map.104 = (f32[112,512]{1,0:T(8,128)}, f32[16,1,512]{2,1,0:T(1,128)}) custom-call(bf16[32,3200]{1,0:T(8,128)(2,1)} %bitcast.9, bf16[100,512]{1,0:T(8,128)(2,1)} %w_own.1, f32[16,1,512]{2,1,0:T(1,128)} %bitcast.10, s32[1,512]{1,0:T(1,128)} %places.1, s32[1,3200]{1,0:T(1,128)} %bitcast.11, f32[1,3200]{1,0:T(1,128)} %bitcast.12, f32[1,512]{1,0:T(1,128)} %column_draws.1, ...), custom_call_target="tpu_custom_call" | custom-call | tf_op jit(solution)/shard_map/pallas_call | solution.py:701
  120.4 1.7 %shard_map.105 = (f32[100,512]{1,0:T(8,128)}, f32[16,1,512]{2,1,0:T(1,128)}) custom-call(f32[112,512]{1,0:T(8,128)} %get-tuple-element.6.summed, f32[16,1,512]{2,1,0:T(1,128)} %get-tuple-element.7.gain), custom_call_target="tpu_custom_call" | custom-call | tf_op jit(solution)/shard_map/pallas_call | solution.py:724

commit v5 on v4

--- a/solution.py
+++ b/solution.py
@@ -299,13 +299,13 @@
 
     row_chunks = tok // 16
     w_done = min(5, h)
-    at_step(1, lambda: text_part(0, row_chunks // 2))
+    for i in range(4):
+        at_step(1 + i, functools.partial(text_part, row_chunks * i // 4, row_chunks * (i + 1) // 4))
     at_step(1, w_second)
-    at_step(2, lambda: text_part(row_chunks // 2, row_chunks))
-    at_step(2, send_text_gain)
+    at_step(4, send_text_gain)
     at_step(3, w_third)
-    at_step(3, bucket_columns)
-    at_step(min(4, h - 1), token_picks)
+    at_step(6, bucket_columns)
+    at_step(min(3, h - 1), token_picks)
     at_step(w_done, w_last)
     for g in sorted(range(groups), key=lambda g: done_at[g]):
         at_step(max(done_at[g], w_done), functools.partial(token_rows, g))
@@ -545,7 +545,7 @@
 
     pairs = ny // 2
     steps = nx * pairs
-    beside = {1: gain_second, 2: gain_third, 3: gain_fourth}
+    beside = ((1, gain_second), (2, gain_third), (3, gain_fourth))
 
     def pair_of(t):
         return 1 + t // pairs, 2 * lax.rem(t, pairs) + 1
@@ -559,8 +559,8 @@
         swap(k, j).start()
         quantize(base_q + y_at(j + 1), 1)
         swap(k, j + 1).start()
-        for at, job in beside.items():
-            pl.when(t == at * pairs - 1)(job)
+        for at, job in beside:
+            pl.when(t == min(at * pairs, steps) - 1)(job)
 
         @pl.when(t > 0)
         def before():

time: 123 us -> 123 us (level)
  no operation moved by 1% of the time
where the time goes in v5:
time: 123 us; the launch traced here: 122 us
  Pallas kernels  121 us (98%)
    pallas_call x1, Pallas kernels, on_device(): pl.pallas_call(functools.partial(kernel, sizes), out_shape=(jax.ShapeDtyp...  120 us

profile of v5, /device:TPU:1, one launch (start us, length us, event | category | flops | bytes accessed | tf_op | source)
XLA Modules:
  0.0 122.1 jit_solution(6635104049189816759)
XLA Ops:
  0.6 119.8 %shard_map.104 = (f32[112,512]{1,0:T(8,128)}, f32[16,1,512]{2,1,0:T(1,128)}) custom-call(bf16[32,3200]{1,0:T(8,128)(2,1)} %bitcast.9, bf16[100,512]{1,0:T(8,128)(2,1)} %w_own.1, f32[16,1,512]{2,1,0:T(1,128)} %bitcast.10, s32[1,512]{1,0:T(1,128)} %places.1, s32[1,3200]{1,0:T(1,128)} %bitcast.11, f32[1,3200]{1,0:T(1,128)} %bitcast.12, f32[1,512]{1,0:T(1,128)} %column_draws.1, ...), custom_call_target="tpu_custom_call" | custom-call | tf_op jit(solution)/shard_map/pallas_call | solution.py:701
  120.4 1.7 %shard_map.105 = (f32[100,512]{1,0:T(8,128)}, f32[16,1,512]{2,1,0:T(1,128)}) custom-call(f32[112,512]{1,0:T(8,128)} %get-tuple-element.6.summed, f32[16,1,512]{2,1,0:T(1,128)} %get-tuple-element.7.gain), custom_call_target="tpu_custom_call" | custom-call | tf_op jit(solution)/shard_map/pallas_call | solution.py:724
